TPU v7x, 32 devices: a whole 2x2x4 slice. The times are simulated.
32 devices in a mesh: pre: 2 (over core), dec: 4 (over z), head: 4 (over y, x).
Axes of the slice: x: 2, y: 2, z: 4, core: 2. Of those that a mesh axis runs over, the one named last changes fastest.
Arguments:
- prompt_query: bfloat16 [2, 4096, 32, 128], P('pre', 'dec', 'head'), may hold values from -6 to 6
- prompt_key: bfloat16 [2, 4096, 32, 128], P('pre', 'dec', 'head'), may hold values from -6 to 6
- prompt_value: bfloat16 [2, 4096, 32, 128], P('pre', 'dec', 'head'), may hold values from -6 to 6
- prompt_beta: float32 [2, 32, 4096], P('pre', 'head', 'dec'), may hold values from 0.05 to 0.95
- prompt_gate: float32 [2, 32, 4096], P('pre', 'head', 'dec')
- prompt_lengths: int32 [2, 4], P('pre'), may hold values from 1 to 32, 64 in all within a row
- request_source_prompt: int32 [128], replicated, may hold values from 0 to 7
- live_counts: int32 [8], P(('pre', 'dec')), may hold values from 1 to 16, as said below
- decode_query: bfloat16 [128, 4, 32, 128], P(('pre', 'dec'), None, 'head'), may hold values from -6 to 6
- decode_key: bfloat16 [128, 4, 32, 128], P(('pre', 'dec'), None, 'head'), may hold values from -6 to 6
- decode_value: bfloat16 [128, 4, 32, 128], P(('pre', 'dec'), None, 'head'), may hold values from -6 to 6
- decode_beta: bfloat16 [128, 4, 32], P(('pre', 'dec'), None, 'head'), may hold values from 0.049804688 to 0.94921875
- decode_gate: bfloat16 [128, 4, 32], P(('pre', 'dec'), None, 'head'), may hold values from -0.69921875 to -0.019897461
Outputs:
- prompt_output: bfloat16 [2, 4096, 32, 128], P('pre', 'dec', 'head')
- step_output: bfloat16 [128, 4, 32, 128], P(('pre', 'dec'), None, 'head')
Inputs may be any that keep to these rules, and one draw needn't show every extreme that they name: `prompt_lengths`: prompts are packed in order and fill each sequence exactly; in every sequence the longest prompt has 4096 // 128 blocks. `live_counts`: some decoding device has all 16 slots live in every draw; live slots of a device are its first ones.
All inputs are finite; a program needn't handle non-finite values.
Results may differ from a plain program's by a relative error of at most 0.0061.
Values may be sent and summed in bfloat16 or wider, within the bound.
No kernel may reach another device: no remote copies, remote signals or barrier semaphores. Data moves between devices by JAX's collectives and lax.ppermute only.
A program may use at most 128 MiB of HBM per device.

v0:
```python
import math

import jax
import jax.numpy as jnp
from jax import lax
from jax.sharding import PartitionSpec as P

SPAN = 64
PROMPTS = 4


exact_dots = lax.Precision.HIGHEST


def passed_along(array, axis, by):
    peers = lax.axis_size(axis)
    pairs = [(i, i + by) for i in range(peers) if 0 <= i + by < peers]
    return lax.ppermute(array, axis, pairs)


def unit_rows(source):
    widened = source.astype(jnp.float32)
    return widened * lax.rsqrt(jnp.sum(widened * widened, axis=-1, keepdims=True) + 1e-06)


def inverse_norms(source):
    widened = source.astype(jnp.float32)
    return jnp.transpose(lax.rsqrt(jnp.sum(widened * widened, axis=-1) + 1e-06), (0, 2, 1))


def product(left, right):
    return jnp.matmul(left, right, precision=exact_dots)


def span_terms(query_rows, key_rows, values, beta_rows, log_gate):
    block_size = key_rows.shape[1]
    q_unit = unit_rows(query_rows)
    k_unit = unit_rows(key_rows)
    k_scale = inverse_norms(key_rows)
    q_scale = inverse_norms(query_rows)
    cum_gate = jnp.transpose(jnp.cumsum(log_gate, axis=2), (1, 0, 2))
    betas = jnp.transpose(beta_rows, (1, 0, 2))
    row_ids = lax.broadcasted_iota(jnp.int32, (block_size, block_size), 0)
    col_ids = lax.broadcasted_iota(jnp.int32, (block_size, block_size), 1)
    on_lower = row_ids >= col_ids
    log_gap = jnp.where(on_lower, cum_gate[:, :, :, None] - cum_gate[:, :, None, :], 0.0)
    decays = jnp.where(on_lower, jnp.exp(log_gap), 0.0)
    raw_gram = jnp.einsum("nihd,njhd->nhij", key_rows, key_rows, preferred_element_type=jnp.float32)
    key_gram = raw_gram * k_scale[:, :, :, None] * k_scale[:, :, None, :]
    strict_part = jnp.where(row_ids > col_ids, betas[:, :, :, None] * decays * key_gram, 0.0)
    identity = jnp.eye(block_size, dtype=jnp.float32)
    powered = strict_part
    inverse = identity - strict_part
    for rounds in range(int(math.log2(block_size)) - 1):
        powered = product(powered, powered)
        inverse = product(inverse, identity + powered)
    inverse_half = inverse.astype(jnp.bfloat16)
    growth = jnp.exp(cum_gate)
    weighted = (k_unit * jnp.swapaxes(betas * growth, 1, 2)[..., None]).astype(jnp.bfloat16)
    w_rows = jnp.einsum(
        "nhij,njhd->nhid", inverse_half, weighted, preferred_element_type=jnp.float32
    )
    scaled_values = (values.astype(jnp.float32) * jnp.swapaxes(betas, 1, 2)[..., None]).astype(
        jnp.bfloat16
    )
    u_rows = jnp.einsum(
        "nhij,njhd->nhid", inverse_half, scaled_values, preferred_element_type=jnp.float32
    )
    q_grown = q_unit * jnp.swapaxes(growth, 1, 2)[..., None]
    raw_scores = jnp.einsum(
        "nihd,njhd->nhij", query_rows, key_rows, preferred_element_type=jnp.float32
    )
    scores = raw_scores * q_scale[:, :, :, None] * k_scale[:, :, None, :] * decays
    k_tail = k_unit * jnp.swapaxes(jnp.exp(cum_gate[:, :, -1:] - cum_gate), 1, 2)[..., None]
    span_decay = growth[:, :, -1]
    return (q_grown, scores, w_rows, u_rows, k_tail, span_decay)


def fresh_of(piece, entry):
    return piece[3] - jnp.einsum("hid,hde->hie", piece[2], entry, precision=exact_dots)


def emit_of(piece, entry, fresh_part):
    first = jnp.einsum("ihd,hde->ihe", piece[0], entry, precision=exact_dots)
    return first + jnp.einsum("hij,hje->ihe", piece[1], fresh_part, precision=exact_dots)


def leave_of(piece, entry, fresh_part):
    carried = piece[5][:, None, None] * entry
    return carried + jnp.einsum("ihd,hie->hde", piece[4], fresh_part, precision=exact_dots)


def pass_map(piece, entry_map):
    moved = jnp.einsum("hid,hde->hie", piece[2], entry_map, precision=exact_dots)
    return piece[5][:, None, None] * entry_map - jnp.einsum(
        "ihd,hie->hde", piece[4], moved, precision=exact_dots
    )


def join_chain(dev_map, dev_state, empty_state):

    def relay_turn(turn, arriving):
        sending = product(dev_map, arriving) + dev_state
        return passed_along(sending.astype(jnp.bfloat16), "dec", 1).astype(sending.dtype)

    return lax.fori_loop(0, lax.axis_size("dec") - 1, relay_turn, empty_state)


def decode_rows(projected, k_unit, q_unit, values, betas, gates):
    steps_count = k_unit.shape[1]
    cum_gate = jnp.cumsum(gates.astype(jnp.float32), axis=1)
    strengths = betas.astype(jnp.float32)
    widened = values.astype(jnp.float32)
    key_dots = jnp.einsum("nshd,nthd->nhst", k_unit, k_unit, precision=exact_dots)
    query_dots = jnp.einsum("nthd,nshd->nhts", q_unit, k_unit, precision=exact_dots)
    updates = []
    outputs = []
    for moment in range(steps_count):
        growth = jnp.exp(cum_gate[:, moment])[..., None]
        predicted = growth * projected[:, moment]
        for earlier in range(moment):
            weight = (
                jnp.exp(cum_gate[:, moment] - cum_gate[:, earlier])
                * key_dots[:, :, earlier, moment]
            )
            predicted = predicted + weight[..., None] * updates[earlier]
        updates.append(strengths[:, moment, :, None] * (widened[:, moment] - predicted))
        emitted = growth * projected[:, steps_count + moment]
        for earlier in range(moment + 1):
            weight = (
                jnp.exp(cum_gate[:, moment] - cum_gate[:, earlier])
                * query_dots[:, :, moment, earlier]
            )
            emitted = emitted + weight[..., None] * updates[earlier]
        outputs.append(emitted)
    return jnp.stack(outputs, axis=1)


def local(
    prompt_query,
    prompt_key,
    prompt_value,
    prompt_beta,
    prompt_gate,
    prompt_lengths,
    request_source_prompt,
    live_counts,
    decode_query,
    decode_key,
    decode_value,
    decode_beta,
    decode_gate,
):
    tokens = prompt_query.shape[1]
    head_count = prompt_query.shape[2]
    key_width = prompt_key.shape[3]
    value_width = prompt_value.shape[3]
    span_count = tokens // SPAN
    span_parts = span_terms(
        prompt_query.reshape(span_count, SPAN, head_count, key_width),
        prompt_key.reshape(span_count, SPAN, head_count, key_width),
        prompt_value.reshape(span_count, SPAN, head_count, value_width),
        prompt_beta.reshape(head_count, span_count, SPAN),
        prompt_gate.reshape(head_count, span_count, SPAN),
    )
    lengths = prompt_lengths[0]
    end_spans = jnp.cumsum(lengths) - 1
    starts = end_spans + 1 - lengths
    span_ids = lax.axis_index("dec") * span_count + jnp.arange(span_count, dtype=jnp.int32)
    keep_flags = 1.0 - jnp.any(span_ids[:, None] == starts[None, :], axis=1).astype(jnp.float32)
    identity = jnp.broadcast_to(
        jnp.eye(key_width, dtype=jnp.float32), (head_count, key_width, key_width)
    )
    empty_state = jnp.zeros((head_count, key_width, value_width), jnp.float32)
    empty_table = jnp.zeros((PROMPTS, head_count, key_width, value_width), jnp.float32)

    def map_pass(carry, slices):
        moved, state = carry
        piece, keep = slices
        entry = keep * state
        fresh_part = fresh_of(piece, entry)
        return ((pass_map(piece, keep * moved), leave_of(piece, entry, fresh_part)), keep)

    device_maps, flags_seen = lax.scan(map_pass, (identity, empty_state), (span_parts, keep_flags))
    incoming = join_chain(device_maps[0], device_maps[1], empty_state)

    def true_pass(carry, slices):
        state, end_table = carry
        piece, keep, span_id = slices
        entry = keep * state
        fresh_part = fresh_of(piece, entry)
        output = emit_of(piece, entry, fresh_part)
        leaving = leave_of(piece, entry, fresh_part)
        hit = (end_spans == span_id)[:, None, None, None]
        end_table = jnp.where(hit, leaving[None], end_table)
        return ((leaving, end_table), output)

    finals, outputs = lax.scan(
        true_pass, (incoming, empty_table), (span_parts, keep_flags, span_ids)
    )
    end_table = finals[1]
    prompt_result = outputs.reshape(1, tokens, head_count, value_width).astype(jnp.bfloat16)
    local_table = lax.psum(end_table.astype(jnp.bfloat16), "dec")
    slot_count = decode_query.shape[0]
    live_slots = jnp.arange(slot_count, dtype=jnp.int32) < live_counts[0]
    dec_count = lax.axis_size("dec")
    whole = lax.all_gather(local_table, "pre", axis=0, tiled=True)
    own_start = (lax.axis_index("pre") * dec_count + lax.axis_index("dec")) * slot_count
    own_ids = lax.dynamic_slice_in_dim(request_source_prompt, own_start, slot_count)
    starting = jnp.take(whole, own_ids, axis=0).astype(jnp.float32)
    k_unit = unit_rows(decode_key)
    q_unit = unit_rows(decode_query)
    probes = jnp.concatenate([k_unit, q_unit], axis=1)
    projected = jnp.einsum("nshd,nhde->nshe", probes, starting, precision=exact_dots)
    own_rows = decode_rows(projected, k_unit, q_unit, decode_value, decode_beta, decode_gate)
    decode_result = jnp.where(live_slots[:, None, None, None], own_rows, 0.0).astype(jnp.bfloat16)
    return (prompt_result, decode_result)


def solution(mesh):
    in_specs = (
        P("pre", "dec", "head", None),
        P("pre", "dec", "head", None),
        P("pre", "dec", "head", None),
        P("pre", "head", "dec"),
        P("pre", "head", "dec"),
        P("pre", None),
        P(),
        P(("pre", "dec")),
        P(("pre", "dec"), None, "head", None),
        P(("pre", "dec"), None, "head", None),
        P(("pre", "dec"), None, "head", None),
        P(("pre", "dec"), None, "head"),
        P(("pre", "dec"), None, "head"),
    )
    out_specs = (P("pre", "dec", "head", None), P(("pre", "dec"), None, "head", None))
    return jax.shard_map(local, mesh=mesh, in_specs=in_specs, out_specs=out_specs, check_vma=False)
```

profile of v0, /device:TPU:0, one launch (start us, length us, event | category | flops | bytes accessed | tf_op | source)
XLA Modules:
  0.0 586.6 jit_solution(12260564706461636411)
XLA Ops:
  11.6 2.8 multiply_reduce_fusion.1
  15.0 6.0 %multiply_select_fusion = f32[16,8,64,64]{3,2,1,0:T(8,128)S(1)} fusion(f32[16,8,64]{2,1,0:T(8,128)S(1)} %copy.286, f32[16,8,64]{2,1,0:T(8,128)S(1)} %copy.282, f32[16,8,64]{2,1,0:T(8,128)S(1)} %copy.281, pred[64,64]{1,0:T(8,128)(4,1)S(1)} %get-tuple-element.438, pred[64,64]{1,0:T(8,128)(4,1)S(1)} %get-tuple-element.439, bf16[16,64,8,128]{3,2,1,0:T(8,128)(2,1)} %bitcast.213), kind=kOutput, calls=%fused_computation.76 | convolution fusion | flops 138412032 | bytes 4300800 | tf_op jit(solution)/shard_map/nihd,njhd->nhij/dot_general | solution.py:48
  21.0 5.5 fusion.119
  26.5 5.5 fusion.120
  32.0 6.0 %fusion.53 = f32[16,8,64,64]{3,2,1,0:T(8,128)S(1)} fusion(f32[16,8,64,64]{3,2,1,0:T(8,128)S(1)} %fusion.119, f32[16,8,64,64]{3,2,1,0:T(8,128)S(1)} %multiply_select_fusion, f32[64,64]{1,0:T(8,128)S(1)} %fusion.108), kind=kOutput, calls=%fused_computation.73 | convolution fusion | flops 403701760 | bytes 6307840 | tf_op jit(solution)/shard_map/dot_general | solution.py:32
  38.0 5.5 fusion.121
  43.5 5.6 fusion.51
  49.1 5.5 fusion.122
  54.6 5.4 fusion.49
  60.0 6.1 %fusion.123 = f32[16,8,64,64]{3,2,1,0:T(8,128)} fusion(f32[16,8,64,64]{3,2,1,0:T(8,128)S(1)} %fusion.122), kind=kOutput, calls=%fused_computation.209 | convolution fusion | flops 402653184 | bytes 4194304 | tf_op jit(solution)/shard_map/dot_general | solution.py:32
  66.1 5.8 fusion.47
  74.7 4.1 convert.1
  78.9 5.1 multiply_convert_fusion
  87.0 8.4 %fusion.70 = bf16[16,8,64,64]{3,2,1,0:T(8,128)(2,1)S(1)} fusion(f32[16,8,64,64]{3,2,1,0:T(8,128)} %fusion.47, f32[16,8,64,64]{3,2,1,0:T(8,128)} %fusion.123, f32[64,64]{1,0:T(8,128)S(1)} %fusion.108), kind=kOutput, calls=%fused_computation.93 | convolution fusion | flops 403701760 | bytes 5259264 | tf_op jit(solution)/shard_map/dot_general | solution.py:32
  95.4 2.8 fusion.61
  98.9 2.8 fusion.58
  101.8 169.1 %while.39 = (s32[]{:T(128)}, f32[8,128,128]{2,1,0:T(8,128)S(1)}, f32[8,128,128]{2,1,0:T(8,128)S(1)}, f32[16,8]{1,0:T(8,128)S(1)}, f32[16]{0:T(128)S(1)}, /*index...) while((s32[]{:T(128)}, f32[8,128,128]{2,1,0:T(8,128)S(1)}, ...), condition=%wide.region_5.6_spmd.clone, body=%wide.region_4.0_spmd.clone.sunk | while | flops 404029440 | bytes 5509888 | solution.py:184
  270.9 2.8 multiply_reduce_fusion
  275.3 5.4 multiply_multiply_fusion
  280.7 3.9 multiply_multiply_fusion.1
  284.6 29.9 %while.40 = (s32[]{:T(128)}, f32[8,128,128]{2,1,0:T(8,128)S(1)}, f32[8,128,128]{2,1,0:T(8,128)S(1)}, f32[8,128,128]{2,1,0:T(8,128)S(1)}, s32[]{:T(128)}, /*index=5*/s32[]{:T(128)}) while((s32[]{:T(128)}, f32[8,128,128]{2,1,0:T(8,128)S(1)}, f32[8,128,128]{2,1,0:T(8,128)S(1)}, f32[8,128,128]{2,1,0:T(8,128)S(1)}, s32[]{:T(128)}, ...), condition=%wide.region_7.8_spmd.clone, body=%wide.region_6.7_spmd.clone.sunk | while | flops 201850880 | bytes 3670135 | solution.py:106
  285.2 4.9 collective-permute-start
  290.2 5.5 collective-permute-done
  296.4 4.4 collective-permute-start
  300.8 4.7 collective-permute-done
  306.2 4.4 collective-permute-start
  310.6 3.9 collective-permute-done
  314.5 184.7 %while.41 = (s32[]{:T(128)}, f32[8,128,128]{2,1,0:T(8,128)S(1)}, bf16[4,8,128,128]{3,2,1,0:T(8,128)(2,1)S(1)}, bf16[16,64,8,128]{3,1,2,0:T(8,128)(2,1)}, f32[16,...) while((s32[]{:T(128)}, f32[8,128,128]{2,1,0:T(8,128)S(1)}, ...), condition=%wide.region_10.11_spmd.clone, body=%wide.region_9.10_spmd.clone.sunk | while | flops 354156544 | bytes 8130359 | solution.py:198
  508.5 45.8 %all-reduce.2.cloned.1.call-done = bf16[4,8,128,128]{3,2,1,0:T(8,128)(2,1)} async-done(((bf16[4,8,128,128]{3,2,1,0:T(8,128)(2,1)}), bf16[4,8,128,128]{3,2,1,0:T(8,128)(2,1)}) %all-reduce.2.cloned.1.call-update) | async-done | bytes 1048592 | tf_op jit(solution)/shard_map/psum | solution.py:203
  563.8 3.1 copy.303
  568.0 4.6 gather_fusion
  572.7 5.2 fusion.43
  (402 shorter events, 387.4 us)
Async XLA Ops:
  7.2 7.7 %copy-start.15 = (f32[1,8,1024]{2,1,0:T(8,128)S(1)}, f32[1,8,1024]{2,1,0:T(8,128)}, u32[]{:S(2)}) copy-start(f32[1,8,1024]{2,1,0:T(8,128)} %param.22) | copy-start | bytes 98308
  7.2 547.1 %all-reduce.2.cloned.1.call-start = ((), (), s32[]{:S(2)}) async-start(), calls=%async_computation | async-start | bytes 2097152 | tf_op jit(solution)/shard_map/psum | solution.py:203
  9.9 11.1 %copy-start.11 = (f32[16,8,64]{2,1,0:T(8,128)}, f32[16,8,64]{2,1,0:T(8,128)S(1)}, u32[]{:S(2)}) copy-start(f32[16,8,64]{2,1,0:T(8,128)S(1)} %copy.282) | copy-start | bytes 98308
  14.9 6.1 %copy-start.13 = (f32[16,8,64]{2,1,0:T(8,128)}, f32[16,8,64]{2,1,0:T(8,128)S(1)}, u32[]{:S(2)}) copy-start(f32[16,8,64]{2,1,0:T(8,128)S(1)} %copy.286) | copy-start | bytes 98308
  74.7 4.2 copy-start.2
  74.7 4.2 copy-start.6
  87.0 8.4 %copy-start.4 = (bf16[16,64,8,128]{3,2,1,0:T(8,128)(2,1)S(1)}, bf16[16,64,8,128]{3,2,1,0:T(8,128)(2,1)}, u32[]{:S(2)}) copy-start(bf16[16,64,8,128]{3,2,1,0:T(8,128)(2,1)} %get-tuple-element.391) | copy-start | bytes 6291460
  95.4 3.5 copy-start.1
  270.9 4.4 copy-start.12
  270.9 4.4 copy-start.14
  275.3 5.4 copy-start.3
  275.3 5.4 copy-start.5
  285.2 10.5 %collective-permute-start = (bf16[8,128,128]{2,1,0:T(8,128)(2,1)S(1)}, bf16[8,128,128]{2,1,0:T(8,128)(2,1)S(1)}, u32[]{:S(2)}, u32[]{:S(2)}) collective-permute-start(bf16[8,128,128]{2,1,0:T(8,128)(2,1)S(1)} %fusion.178), channel_id=1, source_target_pairs={{0,4},{4,8},{8,12},{1,5},{5,9},{9,13},{2,6},{6,10},{10,14},{3,7},{... | collective-permute-start | bytes 786440 | tf_op jit(solution)/shard_map/while/body/eval_jaxpr/ppermute | solution.py:18
  296.4 9.1 %collective-permute-start = (bf16[8,128,128]{2,1,0:T(8,128)(2,1)S(1)}, bf16[8,128,128]{2,1,0:T(8,128)(2,1)S(1)}, u32[]{:S(2)}, u32[]{:S(2)}) collective-permute-start(bf16[8,128,128]{2,1,0:T(8,128)(2,1)S(1)} %fusion.178), channel_id=1, source_target_pairs={{0,4},{4,8},{8,12},{1,5},{5,9},{9,13},{2,6},{6,10},{10,14},{3,7},{... | collective-permute-start | bytes 786440 | tf_op jit(solution)/shard_map/while/body/eval_jaxpr/ppermute | solution.py:18
  306.2 8.3 %collective-permute-start = (bf16[8,128,128]{2,1,0:T(8,128)(2,1)S(1)}, bf16[8,128,128]{2,1,0:T(8,128)(2,1)S(1)}, u32[]{:S(2)}, u32[]{:S(2)}) collective-permute-start(bf16[8,128,128]{2,1,0:T(8,128)(2,1)S(1)} %fusion.178), channel_id=1, source_target_pairs={{0,4},{4,8},{8,12},{1,5},{5,9},{9,13},{2,6},{6,10},{10,14},{3,7},{... | collective-permute-start | bytes 786440 | tf_op jit(solution)/shard_map/while/body/eval_jaxpr/ppermute | solution.py:18
  314.5 185.9 %copy-start.9 = (bf16[16,4,8,128]{3,2,1,0:T(8,128)(2,1)S(1)}, bf16[16,4,8,128]{3,2,1,0:T(8,128)(2,1)}, u32[]{:S(2)}) copy-start(bf16[16,4,8,128]{3,2,1,0:T(8,128)(2,1)} %param.28) | copy-start | bytes 393220
  314.5 186.2 %copy-start.8 = (bf16[16,4,8,128]{3,2,1,0:T(8,128)(2,1)S(1)}, bf16[16,4,8,128]{3,2,1,0:T(8,128)(2,1)}, u32[]{:S(2)}) copy-start(bf16[16,4,8,128]{3,2,1,0:T(8,128)(2,1)} %param.27) | copy-start | bytes 393220
  499.2 1.0 copy-start
  499.2 58.3 %copy-start.10 = (bf16[16,4,8,128]{3,2,1,0:T(8,128)(2,1)S(1)}, bf16[16,4,8,128]{3,2,1,0:T(8,128)(2,1)}, u32[]{:S(2)}) copy-start(bf16[16,4,8,128]{3,2,1,0:T(8,128)(2,1)} %param.29) | copy-start | bytes 393220
  500.2 67.8 %all-gather.2.cloned.1.call-start = ((), (), s32[]{:S(2)}) async-start(), calls=%async_computation.1 | async-start | bytes 3145728 | tf_op jit(solution)/shard_map/all_gather | solution.py:207
  500.9 62.9 %copy-start.7 = (bf16[16,64,8,128]{3,1,2,0:T(8,128)(2,1)S(1)}, bf16[16,64,8,128]{3,1,2,0:T(8,128)(2,1)}, u32[]{:S(2)}) copy-start(bf16[16,64,8,128]{3,1,2,0:T(8,128)(2,1)} %get-tuple-element.138) | copy-start | bytes 6291460
Sparse Core Ops, SparseCore 0:
  500.3 53.9 all-reduce.1
  555.9 9.9 all-gather.1
where the time goes:
time: 595 us; the launch traced here: 587 us
  matrix products  375 us (63%)
  local copies, waits for them, and re-layouts  73.6 us (12%)
  waiting for transfers between devices  59.9 us (10%)
  other arithmetic  46.1 us (8%)
  between operations  15.4 us (3%)
  starting transfers between devices  14 us (2%)
    dot_general x32, matrix products, leave_of(): jnp.einsum('ihd,hie->hde', piece[4], fresh_part, precision=exact_dots)  86.9 us
    dot_general x32, matrix products, fresh_of(): jnp.einsum('hid,hde->hie', piece[2], entry, precision=exact_dots)  72.6 us
    dot_general x13, matrix products, product(): return jnp.matmul(left, right, precision=exact_dots)  61.2 us
    psum x1, waiting for transfers between devices, local(): local_table = lax.psum(end_table.astype(jnp.bfloat16), 'dec')  45.8 us
    dot_general x16, matrix products, pass_map(): jnp.einsum('ihd,hie->hde', piece[4], moved, precision=exact_dots)  43.5 us
    dot_general x16, matrix products, pass_map(): jnp.einsum('hid,hde->hie', piece[2], entry_map, precision=exact_dots)  35 us
    dynamic_slice x48, local copies, waits for them, and re-layouts, local(): lax.scan(map_pass, (identity, empty_state), (span_parts, keep_flags))  34.3 us
    dot_general x16, matrix products, emit_of(): jnp.einsum('hij,hje->ihe', piece[1], fresh_part, precision=exact_dots)  31.9 us
  transfers between devices with their start and end apart: 5, of which 4 were waited for; matrix products, arithmetic and copies ran while one was open for 4% of the time, Pallas kernels for 0%

commit v1 on v0

v1 whole, which is shorter than its diff:
```python
import functools

import jax
import jax.numpy as jnp
from jax import lax
from jax.experimental import pallas as pl
from jax.experimental.pallas import tpu as pltpu
from jax.sharding import PartitionSpec as P

SPAN = 64
PROMPTS = 4
F32 = jnp.float32
BF16 = jnp.bfloat16
MIB = 1024 * 1024
VMEM_BYTES = 60 * MIB
BASE = 32
SUBS = 2


def dot(left, right):
    return jnp.dot(left, right, preferred_element_type=F32)


def dot_last(left, right):
    return lax.dot_general(left, right, (((1,), (1,)), ((), ())), preferred_element_type=F32)


def scale_of(rows):
    return lax.rsqrt(jnp.sum(rows * rows, axis=-1, keepdims=True) + 1e-06)


def unit(rows):
    return rows * scale_of(rows)


def iota2(shape, dim):
    return lax.broadcasted_iota(jnp.int32, shape, dim)


def any_equal(marks, value):
    found = marks[0] == value
    for mark in marks[1:]:
        found = jnp.logical_or(found, mark == value)
    return found


def prompt_ends(lengths):
    ends = [lengths[0, 0] - 1]
    for j in range(1, PROMPTS):
        ends.append(ends[-1] + lengths[0, j])
    return ends


def first_end_in(ends, first, count):
    found = jnp.int32(count)
    for end in reversed(ends):
        inside = jnp.logical_and(end >= first, end < first + count)
        found = jnp.where(inside, end - first, found)
    return found


def tiled(part, size):
    return jnp.concatenate([part] * (size // part.shape[0]), axis=0)


def inverse_of(lower, masks, group):
    size = lower[0].shape[0]
    heads = range(group)
    zero = jnp.zeros((size, size), BF16)

    def packed(h, width):
        parts = [
            jnp.where(masks["lanes", width, b], lower[h][b * width : (b + 1) * width], 0.0)
            for b in range(size // width)
        ]
        return functools.reduce(lambda x, y: x + y, parts)

    def spread(part, mask):
        return jnp.where(mask, tiled(part, size), zero)

    small = [packed(h, BASE) for h in heads]
    inverse = [masks["eye"] - small[h] for h in heads]
    part = [small[h].astype(BF16) for h in heads]
    full = [spread(part[h], masks["same", BASE]) for h in heads]
    part = [dot(part[h], full[h]).astype(BF16) for h in heads]
    power = 2
    while power < BASE:
        full = [spread(part[h], masks["same", BASE]) for h in heads]
        if 2 * power < BASE:
            both = [
                dot(jnp.concatenate([part[h], inverse[h].astype(BF16)], axis=0), full[h])
                for h in heads
            ]
            part = [both[h][:BASE].astype(BF16) for h in heads]
            inverse = [inverse[h] + both[h][BASE:] for h in heads]
        else:
            inverse = [inverse[h] + dot(inverse[h].astype(BF16), full[h]) for h in heads]
        power *= 2
    inverse = [inverse[h].astype(BF16) for h in heads]
    full = [spread(inverse[h], masks["same", BASE]) for h in heads]
    width = BASE
    while width < size:
        below = []
        for h in heads:
            parts = [
                jnp.where(
                    masks["lanes", width, 2 * b],
                    lower[h][(2 * b + 1) * width : (2 * b + 2) * width],
                    0.0,
                )
                for b in range(size // (2 * width))
            ]
            below.append(functools.reduce(lambda x, y: x + y, parts).astype(BF16))
        turned = [dot(below[h], full[h]).astype(BF16) for h in heads]
        wide = [spread(turned[h], masks["off", width]) for h in heads]
        corner = [-dot(inverse[h], wide[h]) for h in heads]
        even = masks["even", width]
        corner = [corner[h].astype(BF16) for h in heads]
        inverse = [
            jnp.concatenate(
                [
                    jnp.where(even, inverse[h], jnp.zeros_like(inverse[h])),
                    jnp.where(even, corner[h], inverse[h]),
                ],
                axis=0,
            )
            for h in heads
        ]
        width *= 2
        if width < size:
            full = [spread(inverse[h], masks["same", width]) for h in heads]
    return inverse


def masks_of(size):
    row = iota2((size, size), 0)
    col = iota2((size, size), 1)
    masks = {"eye": (iota2((BASE, size), 0) == iota2((BASE, size), 1) % BASE).astype(F32)}
    width = BASE
    while width < size:
        masks["same", width] = (row // width) == (col // width)
        masks["off", width] = jnp.logical_and(
            (row // (2 * width)) == (col // (2 * width)), (row // width) != (col // width)
        )
        lanes = iota2((width, size), 1) // width
        for b in range(size // width):
            masks["lanes", width, b] = lanes == b
        masks["even", width] = lanes % 2 == 0
        width *= 2
    return masks


def chunk_kernel(
    spans,
    lengths,
    q_ref,
    k_ref,
    v_ref,
    beta_ref,
    gate_ref,
    local_ref,
    probe_ref,
    state_ref,
    sent_ref,
    map_ref,
    table_ref,
    qf,
    kf,
    vf,
    walk,
    fresh,
    turned_keys,
):
    turn = pl.program_id(0)
    block_rows, heads, width = k_ref.shape
    rows = 2 * SPAN
    subs = block_rows // rows
    half = rows // 2
    places = 2 * subs

    @pl.when(turn == 0)
    def _():
        eye = (iota2((width, width), 0) == iota2((width, width), 1)).astype(F32)
        for h in range(heads):
            walk[0, h, :, :width] = jnp.zeros((width, width), F32)
            walk[0, h, :, width:] = eye
        table_ref[...] = jnp.zeros_like(table_ref)

    base = lax.axis_index("dec") * spans
    ends = [end - base for end in prompt_ends(lengths)]
    starts = [-base] + [end + 1 for end in ends[:-1]]
    map_block = jnp.minimum(first_end_in(ends, 0, spans), spans - 1)
    first_place = lax.rem(turn, 2) * subs
    first_block = 2 * subs * turn
    keeps = [
        1.0 - any_equal(starts, first_block + i).astype(F32)
        for i in range(2 * subs)
    ]

    qf[...] = q_ref[...].astype(F32).reshape(block_rows * heads, width)
    kf[...] = k_ref[...].astype(F32).reshape(block_rows * heads, width)
    vf[...] = v_ref[...].astype(F32).reshape(block_rows * heads, width)

    row = iota2((rows, rows), 0)
    col = iota2((rows, rows), 1)
    strict = row > col
    diagonal = row == col
    masks = masks_of(rows)
    lowers, row_opens, lane_opens, totals, total_cols, beta_cols = [], [], [], [], [], []
    for s in range(subs):
        keep1 = keeps[2 * s + 1]
        open_pair = jnp.logical_or(
            (row >= half) == (col >= half), jnp.full((rows, rows), keep1) > 0.5
        )
        lowers.append(jnp.logical_and(row >= col, open_pair))
        row_opens.append(jnp.where(iota2((rows, 1), 0) >= half, keep1, 1.0))
        lane_opens.append(jnp.where(iota2((1, rows), 1) < half, keep1, 1.0))
        total = lax.dot_general(
            gate_ref[:, s * rows : (s + 1) * rows],
            (row <= col).astype(F32),
            (((1,), (0,)), ((), ())),
            precision=lax.Precision.HIGHEST,
            preferred_element_type=F32,
        )
        totals.append(total)
        total_cols.append(jnp.transpose(total))
        beta_cols.append(jnp.transpose(beta_ref[:, s * rows : (s + 1) * rows]))

    units = [(s, h) for s in range(subs) for h in range(heads)]
    idx = range(len(units))

    def rows_of(ref, s, h):
        return ref[pl.ds(s * rows * heads + h, rows, stride=heads), :]

    keys = [rows_of(kf, s, h) for s, h in units]
    queries = [rows_of(qf, s, h) for s, h in units]
    keys_half = [x.astype(BF16) for x in keys]
    queries_half = [x.astype(BF16) for x in queries]
    grams = [
        dot_last(jnp.concatenate([keys_half[i], queries_half[i]], axis=0), keys_half[i])
        for i in idx
    ]
    key_col = [scale_of(keys[i]) for i in idx]
    query_col = [scale_of(queries[i]) for i in idx]
    key_row = [
        lax.rsqrt(
            jnp.sum(jnp.where(diagonal, grams[i][:rows], 0.0), axis=0, keepdims=True) + 1e-06
        )
        for i in idx
    ]
    sums_col = [total_cols[s][:, h : h + 1] for s, h in units]
    sums_row = [totals[s][h : h + 1, :] for s, h in units]
    betas = [beta_cols[s][:, h : h + 1] for s, h in units]
    decays = [
        jnp.exp(jnp.where(lowers[units[i][0]], sums_col[i] - sums_row[i], -1e30)) * key_row[i]
        for i in idx
    ]
    strict_part = [
        jnp.where(strict, (betas[i] * key_col[i]) * (decays[i] * grams[i][:rows]), 0.0)
        for i in idx
    ]
    scores = [(query_col[i] * (decays[i] * grams[i][rows:])).astype(BF16) for i in idx]
    growth = [jnp.exp(sums_col[i]) * row_opens[units[i][0]] for i in idx]
    inverse = inverse_of(strict_part, masks, len(units))
    right = [
        jnp.concatenate(
            [
                (keys[i] * (betas[i] * growth[i] * key_col[i])).astype(BF16),
                (rows_of(vf, *units[i]) * betas[i]).astype(BF16),
            ],
            axis=1,
        )
        for i in idx
    ]
    wu = [dot(inverse[i], right[i]) for i in idx]
    turned = [jnp.transpose(keys[i]) * key_row[i] for i in idx]
    tails = [
        (
            turned[i]
            * (jnp.exp(sums_row[i][:, rows - 1 :] - sums_row[i]) * lane_opens[units[i][0]])
        ).astype(BF16)
        for i in idx
    ]
    grown = [(queries[i] * (growth[i] * query_col[i])).astype(BF16) for i in idx]
    entry = [walk[first_place, h] for h in range(heads)]
    for s in range(subs):
        mine = [s * heads + h for h in range(heads)]
        entry = [x * keeps[2 * s] for x in entry]
        entry_half = [x.astype(BF16) for x in entry]
        moved = [dot(wu[i][:, :width].astype(BF16), entry_half[i % heads]) for i in mine]
        new = [
            jnp.concatenate(
                [
                    wu[i][:, width:] - moved[i % heads][:, :width],
                    -moved[i % heads][:, width:],
                ],
                axis=1,
            ).astype(BF16)
            for i in mine
        ]
        leaving = [
            entry[i % heads] * (jnp.exp(sums_row[i][:, rows - 1 :]) * keeps[2 * s + 1])
            + dot(tails[i], new[i % heads])
            for i in mine
        ]
        outs = [
            dot(
                jnp.concatenate([grown[i], scores[i]], axis=1),
                jnp.concatenate([entry_half[i % heads], new[i % heads]], axis=0),
            )
            for i in mine
        ]
        place = lax.rem(first_place + s + 1, places)
        for h in range(heads):
            walk[place, h] = leaving[h]
            fresh[s, h] = new[h]
            turned_keys[s, h] = turned[mine[h]]
            local_ref[h, s * rows : (s + 1) * rows] = outs[h][:, :width]
            probe_ref[h, s * rows : (s + 1) * rows] = outs[h][:, width:].astype(BF16)
        entry = leaving

    for s in range(subs):
        block0 = first_block + 2 * s
        now = lax.rem(first_place + s, places)
        later = lax.rem(first_place + s + 1, places)

        @pl.when(jnp.logical_or(any_equal(ends, block0), map_block == block0))
        def _(s=s, block0=block0, now=now):
            for h in range(heads):
                row_sums = totals[s][h : h + 1, :]
                at_half = row_sums[:, half - 1 : half]
                lanes = iota2((1, rows), 1)
                weight = jnp.exp(jnp.where(lanes < half, at_half - row_sums, -1e30))
                state = walk[now, h] * (keeps[2 * s] * jnp.exp(at_half)) + dot(
                    (turned_keys[s, h] * weight).astype(BF16), fresh[s, h]
                )
                for j in range(PROMPTS):

                    @pl.when(ends[j] == block0)
                    def _(j=j, h=h, state=state):
                        table_ref[j, h] = state[:, :width].astype(BF16)

                @pl.when(map_block == block0)
                def _(h=h, state=state):
                    map_ref[h] = state[:, width:].astype(BF16)

        for j in range(PROMPTS):

            @pl.when(ends[j] == block0 + 1)
            def _(j=j, later=later):
                table_ref[j] = walk[later, :, :, :width].astype(BF16)

        @pl.when(map_block == block0 + 1)
        def _(later=later):
            map_ref[...] = walk[later, :, :, width:].astype(BF16)

    @pl.when(turn == pl.num_programs(0) - 1)
    def _():
        last = walk[lax.rem(first_place + subs, places), :, :, :width]
        state_ref[...] = last
        sent_ref[...] = last.astype(BF16)


def prefill(lengths, query, key, value, beta, gate):
    tokens, heads, width = key.shape
    rows = 2 * SPAN * SUBS
    token_spec = pl.BlockSpec((rows, heads, width), lambda c, s: (c, 0, 0))
    gate_spec = pl.BlockSpec((heads, rows), lambda c, s: (0, c))
    out_spec = pl.BlockSpec((heads, rows, width), lambda c, s: (0, c, 0))
    whole = pl.BlockSpec((heads, width, width), lambda c, s: (0, 0, 0))
    table_spec = pl.BlockSpec((PROMPTS, heads, width, width), lambda c, s: (0, 0, 0, 0))
    return pl.pallas_call(
        functools.partial(chunk_kernel, tokens // SPAN),
        grid_spec=pltpu.PrefetchScalarGridSpec(
            num_scalar_prefetch=1,
            grid=(tokens // rows,),
            in_specs=[token_spec, token_spec, token_spec, gate_spec, gate_spec],
            out_specs=[out_spec, out_spec, whole, whole, whole, table_spec],
            scratch_shapes=[
                pltpu.VMEM((rows * heads, width), F32),
                pltpu.VMEM((rows * heads, width), F32),
                pltpu.VMEM((rows * heads, width), F32),
                pltpu.VMEM((2 * SUBS, heads, width, 2 * width), F32),
                pltpu.VMEM((SUBS, heads, 2 * SPAN, 2 * width), BF16),
                pltpu.VMEM((SUBS, heads, width, 2 * SPAN), F32),
            ],
        ),
        out_shape=[
            jax.ShapeDtypeStruct((heads, tokens, width), F32),
            jax.ShapeDtypeStruct((heads, tokens, width), BF16),
            jax.ShapeDtypeStruct((heads, width, width), F32),
            jax.ShapeDtypeStruct((heads, width, width), BF16),
            jax.ShapeDtypeStruct((heads, width, width), BF16),
            jax.ShapeDtypeStruct((PROMPTS, heads, width, width), BF16),
        ],
        compiler_params=pltpu.CompilerParams(vmem_limit_bytes=VMEM_BYTES),
        cost_estimate=pl.CostEstimate(flops=6 * 10**9, bytes_accessed=16 * MIB, transcendentals=0),
        name="chunks",
    )(lengths, query, key, value, beta, gate)


def request_kernel(q_ref, k_ref, v_ref, scale_ref, probe_ref, local_ref, rows_ref):
    slots, steps, heads, width = q_ref.shape
    keys = [unit(k_ref[:, t].astype(F32)) for t in range(steps)]
    queries = [unit(q_ref[:, t].astype(F32)) for t in range(steps)]
    gates = []
    for t in range(steps):
        gate = scale_ref[1, t]
        gates.append(gate if t == 0 else gates[-1] + gate)
    weights, updates = [], []
    for t in range(steps):
        beta = scale_ref[0, t]
        reach = jnp.exp(gates[t]) * keys[t]
        value = v_ref[:, t].astype(F32)
        for s in range(t):
            factor = jnp.exp(gates[t] - gates[s]) * jnp.sum(keys[s] * keys[t], axis=-1, keepdims=True)
            reach = reach - factor * weights[s]
            value = value - factor * updates[s]
        weights.append(beta * reach)
        updates.append(beta * value)
        probe = jnp.exp(gates[t]) * queries[t]
        emitted = jnp.zeros_like(value)
        for s in range(t + 1):
            factor = jnp.sum(keys[s] * queries[t], axis=-1, keepdims=True)
            factor = factor if s == t else factor * jnp.exp(gates[t] - gates[s])
            probe = probe - factor * weights[s]
            emitted = emitted + factor * updates[s]
        rows_ref[pl.ds(t * slots * heads, slots * heads), :] = probe.reshape(slots * heads, width)
        local_ref[t] = emitted
    for h in range(heads):
        probe_ref[h] = rows_ref[pl.ds(h, steps * slots, stride=heads), :].astype(BF16)


def requests(query, key, value, beta, gate):
    slots, steps, heads, width = query.shape
    scales = jnp.transpose(jnp.stack([beta, gate]).astype(F32), (0, 2, 1, 3))[..., None]
    return pl.pallas_call(
        request_kernel,
        out_shape=[
            jax.ShapeDtypeStruct((heads, steps * slots, width), BF16),
            jax.ShapeDtypeStruct((steps, slots, heads, width), F32),
        ],
        scratch_shapes=[pltpu.VMEM((steps * slots * heads, width), F32)],
        compiler_params=pltpu.CompilerParams(vmem_limit_bytes=VMEM_BYTES),
        name="requests",
    )(query, key, value, scales)


def reversed_bits(value, count):
    bits, turned = count.bit_length() - 1, 0
    for i in range(bits):
        turned |= ((value >> i) & 1) << (bits - 1 - i)
    return turned


def answer_kernel(
    spans,
    lengths,
    state_ref,
    map_ref,
    arrived_ref,
    next_map_ref,
    table_ref,
    probe_ref,
    source_ref,
    sent_ref,
    keep_ref,
    send_ref,
    source_rows,
    left,
    total,
):
    _, peers, _, rows, width = probe_ref.shape
    me, mine = lax.axis_index("dec"), lax.axis_index("pre")
    ends = prompt_ends(lengths)
    base = me * spans
    places = [
        (p, x, lax.rem(mine + p, 2), jnp.bitwise_xor(me, reversed_bits(x, peers)))
        for p in range(2)
        for x in range(peers)
    ]

    @pl.when(pl.program_id(0) == 0)
    def _():
        for i, (_, _, pre, peer) in enumerate(places):
            source_rows[i * rows : (i + 1) * rows, :] = jnp.broadcast_to(
                source_ref[pre, peer], (rows, width)
            )

    for i, (_, _, pre, peer) in enumerate(places):
        left[i * rows : (i + 1) * rows, :] = probe_ref[pre, peer, 0]
    closed = first_end_in(ends, base, spans) < spans
    through = jnp.where(closed, 0.0, 1.0)
    leaving = state_ref[0] + through * dot(map_ref[0], arrived_ref[0])
    leaving_half = leaving.astype(BF16)
    sent_ref[0] = leaving_half
    carried = dot(next_map_ref[0], leaving_half).astype(BF16)
    next_end = base + spans + first_end_in(ends, base + spans, spans)
    next_prompt = jnp.int32(-1)
    for j in range(PROMPTS):
        next_prompt = jnp.where(ends[j] == next_end, mine * PROMPTS + j, next_prompt)
    total[...] = jnp.where(source_rows[...] == next_prompt, dot(left[...], carried), 0.0)
    for j in range(PROMPTS):

        @pl.when(jnp.logical_and(ends[j] >= base, ends[j] < base + spans))
        def _(j=j):
            total[...] = jnp.where(
                source_rows[...] == mine * PROMPTS + j, dot(left[...], table_ref[j, 0]), total[...]
            )

    size = peers * rows
    keep_ref[:, 0] = total[:size].astype(BF16).reshape(peers, rows, width)
    send_ref[:, 0] = total[size:].astype(BF16).reshape(peers, rows, width)


def answers(lengths, spans, state, own_map, arrived, next_map, table, probes, sources):
    _, peers, heads, rows, width = probes.shape
    per_head = pl.BlockSpec((1, width, width), lambda h, s: (h, 0, 0))
    table_spec = pl.BlockSpec((PROMPTS, 1, width, width), lambda h, s: (0, h, 0, 0))
    probe_spec = pl.BlockSpec((2, peers, 1, rows, width), lambda h, s: (0, 0, h, 0, 0))
    out_spec = pl.BlockSpec((peers, 1, rows, width), lambda h, s: (0, h, 0, 0))
    source_spec = pl.BlockSpec((2, peers, rows, 1), lambda h, s: (0, 0, 0, 0))
    out = jax.ShapeDtypeStruct((peers, heads, rows, width), BF16)
    return pl.pallas_call(
        functools.partial(answer_kernel, spans),
        grid_spec=pltpu.PrefetchScalarGridSpec(
            num_scalar_prefetch=1,
            grid=(heads,),
            in_specs=[per_head] * 4 + [table_spec, probe_spec, source_spec],
            out_specs=[per_head, out_spec, out_spec],
            scratch_shapes=[
                pltpu.VMEM((2 * peers * rows, width), jnp.int32),
                pltpu.VMEM((2 * peers * rows, width), BF16),
                pltpu.VMEM((2 * peers * rows, width), F32),
            ],
        ),
        out_shape=[jax.ShapeDtypeStruct((heads, width, width), BF16), out, out],
        compiler_params=pltpu.CompilerParams(vmem_limit_bytes=VMEM_BYTES),
        name="answers",
    )(lengths, state, own_map, arrived, next_map, table, probes, sources)


def emit_kernel(local_ref, probe_ref, entry_ref, out_ref, rows_ref):
    heads, rows, width = local_ref.shape
    for h in range(heads):
        rows_ref[pl.ds(h, rows, stride=heads), :] = local_ref[h] + dot(probe_ref[h], entry_ref[h])
    out_ref[...] = rows_ref[...].reshape(rows, heads, width).astype(BF16)


def emit(local, probe, entry):
    heads, tokens, width = local.shape
    rows = 2 * SPAN
    spec = pl.BlockSpec((heads, rows, width), lambda c: (0, c, 0))
    return pl.pallas_call(
        emit_kernel,
        grid=(tokens // rows,),
        in_specs=[spec, spec, pl.BlockSpec((heads, width, width), lambda c: (0, 0, 0))],
        out_specs=pl.BlockSpec((rows, heads, width), lambda c: (c, 0, 0)),
        out_shape=jax.ShapeDtypeStruct((tokens, heads, width), BF16),
        scratch_shapes=[pltpu.VMEM((rows * heads, width), F32)],
        compiler_params=pltpu.CompilerParams(vmem_limit_bytes=VMEM_BYTES),
        cost_estimate=pl.CostEstimate(flops=10**9, bytes_accessed=8 * MIB, transcendentals=0),
        name="emit",
    )(local, probe, entry)


def finish_kernel(live, mine_ref, theirs_ref, local_ref, out_ref, rows_ref):
    slots, steps, heads, width = out_ref.shape
    for h in range(heads):
        rows_ref[pl.ds(h, steps * slots, stride=heads), :] = mine_ref[h].astype(F32) + theirs_ref[
            h
        ].astype(F32)
    on = iota2((slots, heads, width), 0) < live[0]
    for t in range(steps):
        part = rows_ref[pl.ds(t * slots * heads, slots * heads), :].reshape(slots, heads, width)
        out_ref[:, t] = jnp.where(on, part + local_ref[t], 0.0).astype(BF16)


def finish(live, mine, theirs, local):
    steps, slots, heads, width = local.shape
    return pl.pallas_call(
        finish_kernel,
        grid_spec=pltpu.PrefetchScalarGridSpec(
            num_scalar_prefetch=1,
            grid=(1,),
            in_specs=[
                pl.BlockSpec(mine.shape, lambda i, s: (0, 0, 0)),
                pl.BlockSpec(mine.shape, lambda i, s: (0, 0, 0)),
                pl.BlockSpec(local.shape, lambda i, s: (0, 0, 0, 0)),
            ],
            out_specs=pl.BlockSpec((slots, steps, heads, width), lambda i, s: (0, 0, 0, 0)),
            scratch_shapes=[pltpu.VMEM((steps * slots * heads, width), F32)],
        ),
        out_shape=jax.ShapeDtypeStruct((slots, steps, heads, width), BF16),
        compiler_params=pltpu.CompilerParams(vmem_limit_bytes=VMEM_BYTES),
        name="finish",
    )(live, mine, theirs, local)


def shifted(array, by):
    peers = lax.axis_size("dec")
    return lax.ppermute(array, "dec", [(i, i + by) for i in range(peers) if 0 <= i + by < peers])


def added(left, right):
    return (left.astype(F32) + right.astype(F32)).astype(BF16)


def local(
    prompt_query,
    prompt_key,
    prompt_value,
    prompt_beta,
    prompt_gate,
    prompt_lengths,
    request_source_prompt,
    live_counts,
    decode_query,
    decode_key,
    decode_value,
    decode_beta,
    decode_gate,
):
    peers = lax.axis_size("dec")
    tokens = prompt_query.shape[1]
    spans = tokens // SPAN
    steps = decode_query.shape[1]
    longest = peers * spans // 2
    hops = max(1, (longest - 2) // spans + 1)
    probes, decode_local = requests(decode_query, decode_key, decode_value, decode_beta, decode_gate)
    probes, prompt_key = lax.optimization_barrier((probes, prompt_key))
    all_probes = lax.all_gather(probes, ("pre", "dec"), axis=0, tiled=False)
    all_probes = all_probes.reshape((2, peers) + probes.shape)
    sources = request_source_prompt.reshape(2, peers, 1, -1)
    slots = sources.shape[3]
    sources = jnp.broadcast_to(sources, (2, peers, steps, slots)).reshape(2, peers, steps * slots, 1)

    chunk_local, chunk_probe, state, sent, own_map, table = prefill(
        prompt_lengths, prompt_query[0], prompt_key[0], prompt_value[0], prompt_beta[0], prompt_gate[0]
    )
    arrived = shifted(sent, 1) if hops > 1 else jnp.zeros_like(sent)
    next_map = shifted(own_map, -1)
    if hops > 2:
        ends = jnp.cumsum(prompt_lengths[0]) - 1
        closed = jnp.any(ends // spans == lax.axis_index("dec"))
        through = jnp.where(closed, 0.0, own_map.astype(F32)).astype(BF16)

        def turn(_, arriving):
            leaving = state + jnp.einsum("hij,hjk->hik", through, arriving, preferred_element_type=F32)
            return shifted(leaving.astype(BF16), 1)

        arrived = lax.fori_loop(0, hops - 2, turn, arrived)
    leaving, keep, send = answers(
        prompt_lengths, spans, state, own_map, arrived, next_map, table, all_probes, sources
    )
    theirs = lax.ppermute(send, "pre", [(0, 1), (1, 0)])
    block = added(keep, theirs)
    bit, part = 1, peers // 2
    while part:
        pairs = [(i, i ^ bit) for i in range(peers)]
        theirs = lax.ppermute(block[part:], "dec", pairs)
        block = block[:part]
        if bit == 1:
            entry = shifted(leaving, 1)
        if part > 1:
            block = added(block, theirs)
        bit, part = 2 * bit, part // 2
    step_result = finish(live_counts, block[0], theirs[0], decode_local)
    prompt_result = emit(chunk_local, chunk_probe, entry)[None]
    return (prompt_result, step_result)


def solution(mesh):
    in_specs = (
        P("pre", "dec", "head", None),
        P("pre", "dec", "head", None),
        P("pre", "dec", "head", None),
        P("pre", "head", "dec"),
        P("pre", "head", "dec"),
        P("pre", None),
        P(),
        P(("pre", "dec")),
        P(("pre", "dec"), None, "head", None),
        P(("pre", "dec"), None, "head", None),
        P(("pre", "dec"), None, "head", None),
        P(("pre", "dec"), None, "head"),
        P(("pre", "dec"), None, "head"),
    )
    out_specs = (P("pre", "dec", "head", None), P(("pre", "dec"), None, "head", None))
    return jax.shard_map(local, mesh=mesh, in_specs=in_specs, out_specs=out_specs, check_vma=False)
```

time: 595 us -> 96.5 us (0.16); the launches traced: 587 us -> 95 us
  matrix products: 375 us -> 0 us
  local copies, waits for them, and re-layouts: 73.6 us -> 4.96 us
  other arithmetic: 46.1 us -> 2.02 us
  Pallas kernels: 0 us -> 43.8 us
  waiting for transfers between devices: 59.9 us -> 17.3 us
    dot_general x148 -> x0, matrix products: 375 us -> none  [the longest x32 86.9 us: leave_of(): jnp.einsum('ihd,hie->hde', piece[4], fresh_part, precision=exact_dots)]
    psum x1 -> x0, waiting for transfers between devices: 45.8 us -> none  [local(): local_table = lax.psum(end_table.astype(jnp.bfloat16), 'dec')]
    pallas_call x0 -> x5, Pallas kernels: none -> 43.8 us  [the longest x1 23.1 us: prefill(): pl.pallas_call(functools.partial(chunk_kernel, tokens // SPAN), grid_spec...]
    dynamic_slice x64 -> x0, local copies, waits for them, and re-layouts: 43.8 us -> none  [the longest x48 34.3 us: local(): lax.scan(map_pass, (identity, empty_state), (span_parts, keep_flags))]
    eq x17 -> x0, other arithmetic: 11 us -> none  [the longest x16 10.4 us: true_pass(): hit = (end_spans == span_id)[:, None, None, None]]
    convert_element_type x10 -> x2, other arithmetic: 10.9 us -> 1.3 us  [added(): return (left.astype(F32) + right.astype(F32)).astype(BF16)]
    select_n x16 -> x0, other arithmetic: 7.42 us -> none  [true_pass(): end_table = jnp.where(hit, leaving[None], end_table)]
    slice x19 -> x2, local copies, waits for them, and re-layouts: 7.58 us -> 0.7 us  [local(): theirs = lax.ppermute(block[part:], 'dec', pairs)]
  transfers between devices with their start and end apart: 5 -> 7, of which waited for: 4 -> 5; matrix products, arithmetic and copies ran while one was open for 4% -> 2% of each run, Pallas kernels for 0% -> 32%
where the time goes in v1:
time: 96.5 us; the launch traced here: 95 us
  Pallas kernels  43.8 us (45%)
  waiting for transfers between devices  17.3 us (18%)
  between operations  14.8 us (15%)
  starting transfers between devices  12.2 us (13%)
  local copies, waits for them, and re-layouts  4.96 us (5%)
  other arithmetic  2.02 us (2%)
    pallas_call x1, Pallas kernels, prefill(): pl.pallas_call(functools.partial(chunk_kernel, tokens // SPAN), grid_spec...  23.1 us
    ppermute x3, waiting for transfers between devices, shifted(): lax.ppermute(array, 'dec', [(i, i + by) for i in range(peers) if 0 <= i +...  10.9 us
    ppermute x3, starting transfers between devices, shifted(): lax.ppermute(array, 'dec', [(i, i + by) for i in range(peers) if 0 <= i +...  9.65 us
    pallas_call x1, Pallas kernels, answers(): pl.pallas_call(functools.partial(answer_kernel, spans), grid_spec=pltpu.P...  8.59 us
    pallas_call x1, Pallas kernels, emit(): pl.pallas_call(emit_kernel, grid=(tokens // rows,), in_specs=[spec, spec,...  7.37 us
    ppermute x2, waiting for transfers between devices, local(): theirs = lax.ppermute(block[part:], 'dec', pairs)  4.63 us
    pallas_call x1, Pallas kernels, requests(): pl.pallas_call(request_kernel, out_shape=[jax.ShapeDtypeStruct((heads, st...  2.89 us
    unnamed x12, local copies, waits for them, and re-layouts  2.05 us
  transfers between devices with their start and end apart: 7, of which 5 were waited for; matrix products, arithmetic and copies ran while one was open for 2% of the time, Pallas kernels for 32%

profile of v1, /device:TPU:0, one launch (start us, length us, event | category | flops | bytes accessed | tf_op | source)
XLA Modules:
  0.0 95.0 jit_solution(15623713028598633975)
XLA Ops:
  7.2 0.0 all-gather.3.cloned.1.call-start
  7.2 0.7 convert_bitcast_fusion
  7.9 1.2 %copy.19.scale_ref = f32[2,4,16,8,1]{4,3,2,1,0:T(8,128)} copy(f32[2,4,16,8,1]{2,3,4,1,0:T(8,128)S(1)} %convert_bitcast_fusion) | data formatting | bytes 8192 | tf_op jit(solution)/shard_map/broadcast_in_dim | solution.py:436
  9.2 2.9 %requests.1 = (bf16[8,64,128]{2,1,0:T(8,128)(2,1)}, f32[4,16,8,128]{3,2,1,0:T(8,128)}) custom-call(bf16[16,4,8,128]{3,2,1,0:T(8,128)(2,1)} %q_ref.1, bf16[16,4,8,128]{3,2,1,0:T(8,128)(2,1)} %k_ref.1, bf16[16,4,8,128]{3,2,1,0:T(8,128)(2,1)} %v_ref.1, f32[2,4,16,8,1]{4,3,2,1,0:T(8,128)} %copy.19.scale_ref), custom_call_target="tpu_custom_call" | custom-call | tf_op jit(solution)/shard_map/requests/pallas_call | solution.py:437
  12.1 0.0 all-gather.3.cloned.1.call-update
  12.1 0.0 copy-start.4
  12.1 23.1 %chunks.1 = (f32[8,1024,128]{2,1,0:T(8,128)}, bf16[8,1024,128]{2,1,0:T(8,128)(2,1)}, f32[8,128,128]{2,1,0:T(8,128)}, bf16[8,128,128]{2,1,0:T(8,128)(2,1)}, bf16[...) custom-call(s32[1,4]{1,0:T(1,128)} %lengths.3, bf16[1024,8,128]{2,1,0:T(8,128)(2,1)} %bitcast.21, ...), custom_call_target="tpu_custom_call" | custom-call | flops 6000000000 | bytes 16777216 | tf_op jit(solution)/shard_map/chunks/pallas_call | solution.py:372
  35.3 5.0 %collective-permute-start = (bf16[8,128,128]{2,1,0:T(8,128)(2,1)}, bf16[8,128,128]{2,1,0:T(8,128)(2,1)S(1)}, u32[]{:S(2)}, u32[]{:S(2)}) collective-permute-start(bf16[8,128,128]{2,1,0:T(8,128)(2,1)} %get-tuple-element.21), channel_id=1, source_target_pairs={{0,4},{4,8},{8,12},{1,5},{5,9},{9,13},{2,6},{6,10},{10,14},{3,7},{... | collective-permute-start | bytes 786440 | tf_op jit(solution)/shard_map/ppermute | solution.py:602
  40.2 1.3 %collective-permute-start.1 = (bf16[8,128,128]{2,1,0:T(8,128)(2,1)}, bf16[8,128,128]{2,1,0:T(8,128)(2,1)S(1)}, u32[]{:S(2)}, u32[]{:S(2)}) collective-permute-start(bf16[8,128,128]{2,1,0:T(8,128)(2,1)} %get-tuple-element.20.map_ref), channel_id=1, source_target_pairs={{4,0},{8,4},{12,8},{5,1},{9,5},{13,9},{6,2},{10,6},{14,10},{7,3},{... | collective-permute-start | bytes 786440 | tf_op jit(solution)/shard_map/ppermute | solution.py:602
  41.5 0.0 copy-done.4
  41.6 0.1 broadcast_in_dim.17
  41.6 0.9 reshape.17.source_ref
  42.5 4.4 %collective-permute-done.arrived_ref = bf16[8,128,128]{2,1,0:T(8,128)(2,1)S(1)} collective-permute-done((bf16[8,128,128]{2,1,0:T(8,128)(2,1)}, bf16[8,128,128]{2,1,0:T(8,128)(2,1)S(1)}, u32[]{:S(2)}, u32[]{:S(2)}) %collective-permute-start) | collective-permute-done | bytes 262176 | tf_op jit(solution)/shard_map/ppermute | solution.py:602
  47.0 4.6 %collective-permute-done.1.next_map_ref = bf16[8,128,128]{2,1,0:T(8,128)(2,1)S(1)} collective-permute-done((bf16[8,128,128]{2,1,0:T(8,128)(2,1)}, bf16[8,128,128]{2,1,0:T(8,128)(2,1)S(1)}, u32[]{:S(2)}, u32[]{:S(2)}) %collective-permute-start.1) | collective-permute-done | bytes 262176 | tf_op jit(solution)/shard_map/ppermute | solution.py:602
  51.5 0.0 copy-done.1
  51.5 0.7 copy-done.2
  52.2 8.6 %answers.1 = (bf16[8,128,128]{2,1,0:T(8,128)(2,1)}, bf16[4,8,64,128]{3,2,1,0:T(8,128)(2,1)}, bf16[4,8,64,128]{3,2,1,0:T(8,128)(2,1)}) custom-call(s32[1,4]{1,0:T(1,128)} %lengths.3, f32[8,128,128]{2,1,0:T(8,128)} %get-tuple-element.19.state_ref, bf16[8,128,128]{2,1,0:T(8,128)(2,1)} %get-tuple-element.20.map_ref, bf16[8,128,128]{2,1,0:T(8,128)(2,1)} %copy-done.1, ...), custom_call_target="tpu_custom_call" | custom-call | tf_op jit(solution)/shard_map/answers/pallas_call | solution.py:524
  60.8 0.9 collective-permute-start.3
  61.7 1.7 %collective-permute-done.3 = bf16[4,8,64,128]{3,2,1,0:T(8,128)(2,1)S(1)} collective-permute-done((bf16[4,8,64,128]{3,2,1,0:T(8,128)(2,1)}, bf16[4,8,64,128]{3,2,1,0:T(8,128)(2,1)S(1)}, u32[]{:S(2)}, u32[]{:S(2)}) %collective-permute-start.3) | collective-permute-done | bytes 524320 | tf_op jit(solution)/shard_map/ppermute | solution.py:656
  63.5 1.2 %add_convert_fusion = bf16[4,8,64,128]{3,2,1,0:T(8,128)(2,1)S(1)} fusion(bf16[4,8,64,128]{3,2,1,0:T(8,128)(2,1)S(1)} %collective-permute-done.3, bf16[4,8,64,128]{3,2,1,0:T(8,128)(2,1)} %get-tuple-element.25), kind=kLoop, calls=%fused_computation | loop fusion | flops 1048576 | bytes 1572864 | tf_op jit(solution)/shard_map/convert_element_type | solution.py:606
  64.7 0.6 collective-permute-start.4
  65.4 3.4 %collective-permute-start.2 = (bf16[8,128,128]{2,1,0:T(8,128)(2,1)S(1)}, bf16[8,128,128]{2,1,0:T(8,128)(2,1)S(1)}, u32[]{:S(2)}, u32[]{:S(2)}) collective-permute-start(bf16[8,128,128]{2,1,0:T(8,128)(2,1)S(1)} %copy-done.5), channel_id=1, source_target_pairs={{0,4},{4,8},{8,12},{1,5},{5,9},{9,13},{2,6},{6,10},{10,14},{3,7},{... | collective-permute-start | bytes 786440 | tf_op jit(solution)/shard_map/ppermute | solution.py:602
  68.8 4.6 %collective-permute-done.4 = bf16[2,8,64,128]{3,2,1,0:T(8,128)(2,1)S(1)} collective-permute-done((bf16[2,8,64,128]{3,2,1,0:T(8,128)(2,1)S(1)}, bf16[2,8,64,128]{3,2,1,0:T(8,128)(2,1)S(1)}, u32[]{:S(2)}, u32[]{:S(2)}) %collective-permute-start.4) | collective-permute-done | bytes 262176 | tf_op jit(solution)/shard_map/ppermute | solution.py:661
  73.4 0.1 add_convert_fusion.1
  73.5 0.7 fusion
  74.2 0.9 collective-permute-start.5
  75.8 1.9 %collective-permute-done.2.entry_ref = bf16[8,128,128]{2,1,0:T(8,128)(2,1)S(1)} collective-permute-done((bf16[8,128,128]{2,1,0:T(8,128)(2,1)S(1)}, bf16[8,128,128]{2,1,0:T(8,128)(2,1)S(1)}, u32[]{:S(2)}, u32[]{:S(2)}) %collective-permute-start.2) | collective-permute-done | bytes 262176 | tf_op jit(solution)/shard_map/ppermute | solution.py:602
  77.6 0.7 copy-done
  78.3 7.4 %emit.1 = bf16[1024,8,128]{2,1,0:T(8,128)(2,1)} custom-call(f32[8,1024,128]{2,1,0:T(8,128)} %get-tuple-element.17.local_ref, bf16[8,1024,128]{2,1,0:T(8,128)(2,1)} %get-tuple-element.18.probe_ref, bf16[8,128,128]{2,1,0:T(8,128)(2,1)} %copy-done), custom_call_target="tpu_custom_call" | custom-call | flops 1000000000 | bytes 8388608 | tf_op jit(solution)/shard_map/emit/pallas_call | solution.py:554
  85.7 0.0 collective-permute-done.5
  85.7 0.6 copy-done.3
  86.4 1.8 %finish.1 = bf16[16,4,8,128]{3,2,1,0:T(8,128)(2,1)} custom-call(s32[1]{0:T(128)S(6)} %copy.21.live, bf16[8,64,128]{2,1,0:T(8,128)(2,1)} %get-tuple-element.29.mine_ref, bf16[8,64,128]{2,1,0:T(8,128)(2,1)} %bitcast.18, f32[4,16,8,128]{3,2,1,0:T(8,128)} %get-tuple-element.27.local_ref), custom_call_target="tpu_custom_call" | custom-call | tf_op jit(solution)/shard_map/finish/pallas_call | solution.py:581
  (9 shorter events, 0.0 us)
Async XLA Ops:
  7.2 44.4 %all-gather.3.cloned.1.call-start = ((), (), s32[]{:S(2)}) async-start(), calls=%async_computation | async-start | bytes 1179648 | tf_op jit(solution)/shard_map/all_gather | solution.py:632
  12.1 29.5 %copy-start.4 = (s32[128]{0:T(128)S(1)}, s32[128]{0:T(128)}, u32[]{:S(2)}) copy-start(s32[128]{0:T(128)} %param.19) | copy-start | bytes 1540
  35.3 11.7 %collective-permute-start = (bf16[8,128,128]{2,1,0:T(8,128)(2,1)}, bf16[8,128,128]{2,1,0:T(8,128)(2,1)S(1)}, u32[]{:S(2)}, u32[]{:S(2)}) collective-permute-start(bf16[8,128,128]{2,1,0:T(8,128)(2,1)} %get-tuple-element.21), channel_id=1, source_target_pairs={{0,4},{4,8},{8,12},{1,5},{5,9},{9,13},{2,6},{6,10},{10,14},{3,7},{... | collective-permute-start | bytes 786440 | tf_op jit(solution)/shard_map/ppermute | solution.py:602
  40.2 11.3 %collective-permute-start.1 = (bf16[8,128,128]{2,1,0:T(8,128)(2,1)}, bf16[8,128,128]{2,1,0:T(8,128)(2,1)S(1)}, u32[]{:S(2)}, u32[]{:S(2)}) collective-permute-start(bf16[8,128,128]{2,1,0:T(8,128)(2,1)} %get-tuple-element.20.map_ref), channel_id=1, source_target_pairs={{4,0},{8,4},{12,8},{5,1},{9,5},{13,9},{6,2},{10,6},{14,10},{7,3},{... | collective-permute-start | bytes 786440 | tf_op jit(solution)/shard_map/ppermute | solution.py:602
  47.0 4.6 %copy-start.1 = (bf16[8,128,128]{2,1,0:T(8,128)(2,1)}, bf16[8,128,128]{2,1,0:T(8,128)(2,1)S(1)}, u32[]{:S(2)}) copy-start(bf16[8,128,128]{2,1,0:T(8,128)(2,1)S(1)} %collective-permute-done.arrived_ref) | copy-start | bytes 786436
  51.5 0.7 copy-start.2
  60.8 4.6 %copy-start.5 = (bf16[8,128,128]{2,1,0:T(8,128)(2,1)S(1)}, bf16[8,128,128]{2,1,0:T(8,128)(2,1)}, u32[]{:S(2)}) copy-start(bf16[8,128,128]{2,1,0:T(8,128)(2,1)} %get-tuple-element.24) | copy-start | bytes 786436
  60.8 2.7 %collective-permute-start.3 = (bf16[4,8,64,128]{3,2,1,0:T(8,128)(2,1)}, bf16[4,8,64,128]{3,2,1,0:T(8,128)(2,1)S(1)}, u32[]{:S(2)}, u32[]{:S(2)}) collective-permute-start(bf16[4,8,64,128]{3,2,1,0:T(8,128)(2,1)} %get-tuple-element.26), channel_id=1, source_target_pairs={{0,16},{16,0},{1,17},{17,1},{2,18},{18,2},{3,19},{19,3},{4,20},{20... | collective-permute-start | bytes 1572872 | tf_op jit(solution)/shard_map/ppermute | solution.py:656
  64.7 8.7 %collective-permute-start.4 = (bf16[2,8,64,128]{3,2,1,0:T(8,128)(2,1)S(1)}, bf16[2,8,64,128]{3,2,1,0:T(8,128)(2,1)S(1)}, u32[]{:S(2)}, u32[]{:S(2)}) collective-permute-start(bf16[2,8,64,128]{3,2,1,0:T(8,128)(2,1)S(1)} %slice.17), channel_id=1, source_target_pairs={{0,4},{4,0},{8,12},{12,8},{1,5},{5,1},{9,13},{13,9},{2,6},{6,2},{1... | collective-permute-start | bytes 786440 | tf_op jit(solution)/shard_map/ppermute | solution.py:661
  65.4 12.3 %collective-permute-start.2 = (bf16[8,128,128]{2,1,0:T(8,128)(2,1)S(1)}, bf16[8,128,128]{2,1,0:T(8,128)(2,1)S(1)}, u32[]{:S(2)}, u32[]{:S(2)}) collective-permute-start(bf16[8,128,128]{2,1,0:T(8,128)(2,1)S(1)} %copy-done.5), channel_id=1, source_target_pairs={{0,4},{4,8},{8,12},{1,5},{5,9},{9,13},{2,6},{6,10},{10,14},{3,7},{... | collective-permute-start | bytes 786440 | tf_op jit(solution)/shard_map/ppermute | solution.py:602
  74.2 11.6 %collective-permute-start.5 = (bf16[1,8,64,128]{3,2,1,0:T(8,128)(2,1)S(1)}, bf16[1,8,64,128]{3,2,1,0:T(8,128)(2,1)S(1)}, u32[]{:S(2)}, u32[]{:S(2)}) collective-permute-start(bf16[1,8,64,128]{3,2,1,0:T(8,128)(2,1)S(1)} %get-tuple-element.28), channel_id=1, source_target_pairs={{0,8},{4,12},{8,0},{12,4},{1,9},{5,13},{9,1},{13,5},{2,10},{6,14},... | collective-permute-start | bytes 393224 | tf_op jit(solution)/shard_map/ppermute | solution.py:661
  77.6 0.7 copy-start
  85.7 0.6 copy-start.3
Sparse Core Ops, SparseCore 0:
  12.2 24.7 all-gather.2

commit v2 on v1

--- a/solution.py
+++ b/solution.py
@@ -13,12 +13,24 @@
 BF16 = jnp.bfloat16
 MIB = 1024 * 1024
 VMEM_BYTES = 60 * MIB
-BASE = 32
+SMALL_BYTES = 16 * MIB
+EMIT_BYTES = 20 * MIB
+CARRIED_MIB = 48
+EMIT_ROWS = 512
+BASE = 64
 SUBS = 2
 
 
 def dot(left, right):
     return jnp.dot(left, right, preferred_element_type=F32)
+
+
+def dot_split(left, right):
+    width = right.shape[1] // 2
+    high = right.astype(BF16)
+    low = (right[:, :width] - high[:, :width].astype(F32)).astype(BF16)
+    both = dot(left, high)
+    return jnp.concatenate([both[:, :width] + dot(left, low), both[:, width:]], axis=1)
 
 
 def dot_last(left, right):
@@ -161,8 +173,8 @@
     local_ref,
     probe_ref,
     state_ref,
-    sent_ref,
-    map_ref,
+    first_ref,
+    second_ref,
     table_ref,
     qf,
     kf,
@@ -170,6 +182,8 @@
     walk,
     fresh,
     turned_keys,
+    half_map,
+    own_map,
 ):
     turn = pl.program_id(0)
     block_rows, heads, width = k_ref.shape
@@ -206,7 +220,7 @@
     strict = row > col
     diagonal = row == col
     masks = masks_of(rows)
-    lowers, row_opens, lane_opens, totals, total_cols, beta_cols = [], [], [], [], [], []
+    lowers, row_opens, tail_opens, totals, total_cols, beta_cols = [], [], [], [], [], []
     for s in range(subs):
         keep1 = keeps[2 * s + 1]
         open_pair = jnp.logical_or(
@@ -214,7 +228,7 @@
         )
         lowers.append(jnp.logical_and(row >= col, open_pair))
         row_opens.append(jnp.where(iota2((rows, 1), 0) >= half, keep1, 1.0))
-        lane_opens.append(jnp.where(iota2((1, rows), 1) < half, keep1, 1.0))
+        tail_opens.append(jnp.where(iota2((rows, 1), 0) < half, keep1, 1.0))
         total = lax.dot_general(
             gate_ref[:, s * rows : (s + 1) * rows],
             (row <= col).astype(F32),
@@ -273,12 +287,9 @@
         for i in idx
     ]
     wu = [dot(inverse[i], right[i]) for i in idx]
-    turned = [jnp.transpose(keys[i]) * key_row[i] for i in idx]
+    turned = [jnp.transpose(keys_half[i]) for i in idx]
     tails = [
-        (
-            turned[i]
-            * (jnp.exp(sums_row[i][:, rows - 1 :] - sums_row[i]) * lane_opens[units[i][0]])
-        ).astype(BF16)
+        jnp.exp(sums_row[i][:, rows - 1 :] - sums_col[i]) * (key_col[i] * tail_opens[units[i][0]])
         for i in idx
     ]
     grown = [(queries[i] * (growth[i] * query_col[i])).astype(BF16) for i in idx]
@@ -295,14 +306,17 @@
                     -moved[i % heads][:, width:],
                 ],
                 axis=1,
-            ).astype(BF16)
+            )
             for i in mine
         ]
+        for h in range(heads):
+            fresh[s, h] = new[h]
         leaving = [
             entry[i % heads] * (jnp.exp(sums_row[i][:, rows - 1 :]) * keeps[2 * s + 1])
-            + dot(tails[i], new[i % heads])
+            + dot_split(turned[i], new[i % heads] * tails[i])
             for i in mine
         ]
+        new = [x.astype(BF16) for x in new]
         outs = [
             dot(
                 jnp.concatenate([grown[i], scores[i]], axis=1),
@@ -313,7 +327,6 @@
         place = lax.rem(first_place + s + 1, places)
         for h in range(heads):
             walk[place, h] = leaving[h]
-            fresh[s, h] = new[h]
             turned_keys[s, h] = turned[mine[h]]
             local_ref[h, s * rows : (s + 1) * rows] = outs[h][:, :width]
             probe_ref[h, s * rows : (s + 1) * rows] = outs[h][:, width:].astype(BF16)
@@ -324,25 +337,27 @@
         now = lax.rem(first_place + s, places)
         later = lax.rem(first_place + s + 1, places)
 
-        @pl.when(jnp.logical_or(any_equal(ends, block0), map_block == block0))
+        @pl.when(any_equal(ends, block0))
         def _(s=s, block0=block0, now=now):
+            prompt = jnp.int32(0)
+            for j in range(1, PROMPTS):
+                prompt = jnp.where(ends[j] == block0, j, prompt)
+            at_half = [totals[s][h : h + 1, half - 1 : half] for h in range(heads)]
+            first_half = iota2((rows, 1), 0) < half
+            weights = [
+                jnp.exp(jnp.where(first_half, at_half[h] - total_cols[s][:, h : h + 1], -1e30))
+                for h in range(heads)
+            ]
+            weights = [weights[h] * scale_of(rows_of(kf, s, h)) for h in range(heads)]
+            steps = [dot_split(turned_keys[s, h], fresh[s, h] * weights[h]) for h in range(heads)]
             for h in range(heads):
-                row_sums = totals[s][h : h + 1, :]
-                at_half = row_sums[:, half - 1 : half]
-                lanes = iota2((1, rows), 1)
-                weight = jnp.exp(jnp.where(lanes < half, at_half - row_sums, -1e30))
-                state = walk[now, h] * (keeps[2 * s] * jnp.exp(at_half)) + dot(
-                    (turned_keys[s, h] * weight).astype(BF16), fresh[s, h]
-                )
-                for j in range(PROMPTS):
-
-                    @pl.when(ends[j] == block0)
-                    def _(j=j, h=h, state=state):
-                        table_ref[j, h] = state[:, :width].astype(BF16)
-
-                @pl.when(map_block == block0)
-                def _(h=h, state=state):
-                    map_ref[h] = state[:, width:].astype(BF16)
+                state = walk[now, h] * (keeps[2 * s] * jnp.exp(at_half[h])) + steps[h]
+                table_ref[prompt, h] = state[:, :width].astype(BF16)
+                half_map[h] = state[:, width:].astype(BF16)
+
+            @pl.when(map_block == block0)
+            def _():
+                own_map[...] = half_map[...]
 
         for j in range(PROMPTS):
 
@@ -352,13 +367,15 @@
 
         @pl.when(map_block == block0 + 1)
         def _(later=later):
-            map_ref[...] = walk[later, :, :, width:].astype(BF16)
+            own_map[...] = walk[later, :, :, width:].astype(BF16)
 
     @pl.when(turn == pl.num_programs(0) - 1)
     def _():
         last = walk[lax.rem(first_place + subs, places), :, :, :width]
         state_ref[...] = last
-        sent_ref[...] = last.astype(BF16)
+        odd = jnp.full(last.shape, lax.rem(lax.axis_index("dec"), 2)) == 1
+        first_ref[...] = jnp.where(odd, own_map[...], last.astype(BF16))
+        second_ref[...] = jnp.where(odd, last.astype(BF16), own_map[...])
 
 
 def prefill(lengths, query, key, value, beta, gate):
@@ -381,8 +398,10 @@
                 pltpu.VMEM((rows * heads, width), F32),
                 pltpu.VMEM((rows * heads, width), F32),
                 pltpu.VMEM((2 * SUBS, heads, width, 2 * width), F32),
-                pltpu.VMEM((SUBS, heads, 2 * SPAN, 2 * width), BF16),
-                pltpu.VMEM((SUBS, heads, width, 2 * SPAN), F32),
+                pltpu.VMEM((SUBS, heads, 2 * SPAN, 2 * width), F32),
+                pltpu.VMEM((SUBS, heads, width, 2 * SPAN), BF16),
+                pltpu.VMEM((heads, width, width), BF16),
+                pltpu.VMEM((heads, width, width), BF16),
             ],
         ),
         out_shape=[
@@ -399,17 +418,24 @@
     )(lengths, query, key, value, beta, gate)
 
 
-def request_kernel(q_ref, k_ref, v_ref, scale_ref, probe_ref, local_ref, rows_ref):
+def request_kernel(q_ref, k_ref, v_ref, beta_ref, gate_ref, probe_ref, local_ref, rows_ref):
     slots, steps, heads, width = q_ref.shape
+
+    def per_slot(ref, t):
+        values = ref[t].astype(F32)
+        return jnp.stack(
+            [jnp.broadcast_to(values[:, i : i + 1], (heads, width)) for i in range(slots)]
+        )
+
     keys = [unit(k_ref[:, t].astype(F32)) for t in range(steps)]
     queries = [unit(q_ref[:, t].astype(F32)) for t in range(steps)]
     gates = []
     for t in range(steps):
-        gate = scale_ref[1, t]
+        gate = per_slot(gate_ref, t)
         gates.append(gate if t == 0 else gates[-1] + gate)
     weights, updates = [], []
     for t in range(steps):
-        beta = scale_ref[0, t]
+        beta = per_slot(beta_ref, t)
         reach = jnp.exp(gates[t]) * keys[t]
         value = v_ref[:, t].astype(F32)
         for s in range(t):
@@ -433,7 +459,7 @@
 
 def requests(query, key, value, beta, gate):
     slots, steps, heads, width = query.shape
-    scales = jnp.transpose(jnp.stack([beta, gate]).astype(F32), (0, 2, 1, 3))[..., None]
+    beta, gate = jnp.transpose(beta, (1, 2, 0)), jnp.transpose(gate, (1, 2, 0))
     return pl.pallas_call(
         request_kernel,
         out_shape=[
@@ -443,7 +469,7 @@
         scratch_shapes=[pltpu.VMEM((steps * slots * heads, width), F32)],
         compiler_params=pltpu.CompilerParams(vmem_limit_bytes=VMEM_BYTES),
         name="requests",
-    )(query, key, value, scales)
+    )(query, key, value, beta, gate)
 
 
 def reversed_bits(value, count):
@@ -453,91 +479,149 @@
     return turned
 
 
-def answer_kernel(
+def reversed_bits(value, count):
+    bits, turned = count.bit_length() - 1, 0
+    for i in range(bits):
+        turned |= ((value >> i) & 1) << (bits - 1 - i)
+    return turned
+
+
+def spread_sources(source_ref, out_ref):
+    _, peers, rows, _ = source_ref.shape
+    me, mine = lax.axis_index("dec"), lax.axis_index("pre")
+    for p in range(2):
+        for x in range(peers):
+            first = (p * peers + x) * rows
+            peer = jnp.bitwise_xor(me, reversed_bits(x, peers))
+            out_ref[first : first + rows, :] = jnp.broadcast_to(
+                source_ref[lax.rem(mine + p, 2), peer], (rows, out_ref.shape[1])
+            )
+
+
+def stored_kernel(spans, lengths, table_ref, own_ref, other_ref, source_ref, keep_ref, send_ref, source_rows, total):
+    peers, _, rows, width = own_ref.shape
+    mine = lax.axis_index("pre")
+    ends = prompt_ends(lengths)
+    base = lax.axis_index("dec") * spans
+    size = peers * rows
+
+    @pl.when(pl.program_id(0) == 0)
+    def _():
+        spread_sources(source_ref, source_rows)
+
+    total[...] = jnp.zeros_like(total)
+    for j in range(PROMPTS):
+
+        @pl.when(jnp.logical_and(ends[j] >= base, ends[j] < base + spans))
+        def _(j=j):
+            for first, ref in ((0, own_ref), (size, other_ref)):
+                rows_here = slice(first, first + size)
+                total[rows_here] = jnp.where(
+                    source_rows[rows_here] == mine * PROMPTS + j,
+                    dot(ref[:, 0].reshape(size, width), table_ref[j, 0]),
+                    total[rows_here],
+                )
+
+    keep_ref[:, 0] = total[:size].astype(BF16).reshape(peers, rows, width)
+    send_ref[:, 0] = total[size:].astype(BF16).reshape(peers, rows, width)
+
+
+def stored_answers(lengths, spans, table, own, other, sources):
+    peers, heads, rows, width = own.shape
+    table_spec = pl.BlockSpec((PROMPTS, 1, width, width), lambda h, s: (0, h, 0, 0))
+    rows_spec = pl.BlockSpec((peers, 1, rows, width), lambda h, s: (0, h, 0, 0))
+    source_spec = pl.BlockSpec((2, peers, rows, 1), lambda h, s: (0, 0, 0, 0))
+    out = jax.ShapeDtypeStruct(own.shape, BF16)
+    return pl.pallas_call(
+        functools.partial(stored_kernel, spans),
+        grid_spec=pltpu.PrefetchScalarGridSpec(
+            num_scalar_prefetch=1,
+            grid=(heads,),
+            in_specs=[table_spec, rows_spec, rows_spec, source_spec],
+            out_specs=[rows_spec, rows_spec],
+            scratch_shapes=[
+                pltpu.VMEM((2 * peers * rows, width), jnp.int32),
+                pltpu.VMEM((2 * peers * rows, width), F32),
+            ],
+        ),
+        out_shape=[out, out],
+        compiler_params=pltpu.CompilerParams(vmem_limit_bytes=16 * MIB),
+        cost_estimate=pl.CostEstimate(flops=10**9, bytes_accessed=16 * MIB, transcendentals=0),
+        name="stored",
+    )(lengths, table, own, other, sources)
+
+
+def carried_kernel(
     spans,
     lengths,
     state_ref,
-    map_ref,
-    arrived_ref,
-    next_map_ref,
-    table_ref,
-    probe_ref,
+    first_ref,
+    second_ref,
+    first_got_ref,
+    second_got_ref,
+    own_ref,
+    other_ref,
+    own_part_ref,
+    other_part_ref,
     source_ref,
     sent_ref,
     keep_ref,
     send_ref,
     source_rows,
-    left,
-    total,
 ):
-    _, peers, _, rows, width = probe_ref.shape
-    me, mine = lax.axis_index("dec"), lax.axis_index("pre")
+    peers, heads, rows, width = own_ref.shape
+    mine = lax.axis_index("pre")
     ends = prompt_ends(lengths)
-    base = me * spans
-    places = [
-        (p, x, lax.rem(mine + p, 2), jnp.bitwise_xor(me, reversed_bits(x, peers)))
-        for p in range(2)
-        for x in range(peers)
-    ]
-
-    @pl.when(pl.program_id(0) == 0)
-    def _():
-        for i, (_, _, pre, peer) in enumerate(places):
-            source_rows[i * rows : (i + 1) * rows, :] = jnp.broadcast_to(
-                source_ref[pre, peer], (rows, width)
-            )
-
-    for i, (_, _, pre, peer) in enumerate(places):
-        left[i * rows : (i + 1) * rows, :] = probe_ref[pre, peer, 0]
-    closed = first_end_in(ends, base, spans) < spans
-    through = jnp.where(closed, 0.0, 1.0)
-    leaving = state_ref[0] + through * dot(map_ref[0], arrived_ref[0])
-    leaving_half = leaving.astype(BF16)
-    sent_ref[0] = leaving_half
-    carried = dot(next_map_ref[0], leaving_half).astype(BF16)
+    base = lax.axis_index("dec") * spans
+    size = peers * rows
+    through = jnp.where(first_end_in(ends, base, spans) < spans, 0.0, 1.0)
     next_end = base + spans + first_end_in(ends, base + spans, spans)
     next_prompt = jnp.int32(-1)
     for j in range(PROMPTS):
         next_prompt = jnp.where(ends[j] == next_end, mine * PROMPTS + j, next_prompt)
-    total[...] = jnp.where(source_rows[...] == next_prompt, dot(left[...], carried), 0.0)
-    for j in range(PROMPTS):
-
-        @pl.when(jnp.logical_and(ends[j] >= base, ends[j] < base + spans))
-        def _(j=j):
-            total[...] = jnp.where(
-                source_rows[...] == mine * PROMPTS + j, dot(left[...], table_ref[j, 0]), total[...]
+    spread_sources(source_ref, source_rows)
+    odd = jnp.full((width, width), lax.rem(lax.axis_index("dec"), 2)) == 1
+    leaving, carried = [], []
+    for h in range(heads):
+        own_map = jnp.where(odd, first_ref[h], second_ref[h])
+        arrived = jnp.where(odd, first_got_ref[h], second_got_ref[h])
+        leaving.append((state_ref[h] + through * dot(own_map, arrived)).astype(BF16))
+    for h in range(heads):
+        next_map = jnp.where(odd, second_got_ref[h], first_got_ref[h])
+        carried.append(dot(next_map, leaving[h]).astype(BF16))
+    for h in range(heads):
+        sent_ref[h] = leaving[h]
+        for first, ref, part, out in (
+            (0, own_ref, own_part_ref, keep_ref),
+            (size, other_ref, other_part_ref, send_ref),
+        ):
+            out[:, h] = (
+                jnp.where(
+                    source_rows[first : first + size] == next_prompt,
+                    dot(ref[:, h].reshape(size, width), carried[h]),
+                    part[:, h].reshape(size, width).astype(F32),
+                )
+                .astype(BF16)
+                .reshape(peers, rows, width)
             )
 
-    size = peers * rows
-    keep_ref[:, 0] = total[:size].astype(BF16).reshape(peers, rows, width)
-    send_ref[:, 0] = total[size:].astype(BF16).reshape(peers, rows, width)
-
-
-def answers(lengths, spans, state, own_map, arrived, next_map, table, probes, sources):
-    _, peers, heads, rows, width = probes.shape
-    per_head = pl.BlockSpec((1, width, width), lambda h, s: (h, 0, 0))
-    table_spec = pl.BlockSpec((PROMPTS, 1, width, width), lambda h, s: (0, h, 0, 0))
-    probe_spec = pl.BlockSpec((2, peers, 1, rows, width), lambda h, s: (0, 0, h, 0, 0))
-    out_spec = pl.BlockSpec((peers, 1, rows, width), lambda h, s: (0, h, 0, 0))
-    source_spec = pl.BlockSpec((2, peers, rows, 1), lambda h, s: (0, 0, 0, 0))
-    out = jax.ShapeDtypeStruct((peers, heads, rows, width), BF16)
+
+def carried_answers(lengths, spans, state, first, second, own, other, own_part, other_part, sources):
+    peers, heads, rows, width = own.shape
+    out = jax.ShapeDtypeStruct(own.shape, BF16)
     return pl.pallas_call(
-        functools.partial(answer_kernel, spans),
+        functools.partial(carried_kernel, spans),
         grid_spec=pltpu.PrefetchScalarGridSpec(
             num_scalar_prefetch=1,
-            grid=(heads,),
-            in_specs=[per_head] * 4 + [table_spec, probe_spec, source_spec],
-            out_specs=[per_head, out_spec, out_spec],
-            scratch_shapes=[
-                pltpu.VMEM((2 * peers * rows, width), jnp.int32),
-                pltpu.VMEM((2 * peers * rows, width), BF16),
-                pltpu.VMEM((2 * peers * rows, width), F32),
-            ],
+            grid=(1,),
+            in_specs=[pl.BlockSpec(memory_space=pltpu.VMEM)] * 10,
+            out_specs=[pl.BlockSpec(memory_space=pltpu.VMEM)] * 3,
+            scratch_shapes=[pltpu.VMEM((2 * peers * rows, width), jnp.int32)],
         ),
         out_shape=[jax.ShapeDtypeStruct((heads, width, width), BF16), out, out],
-        compiler_params=pltpu.CompilerParams(vmem_limit_bytes=VMEM_BYTES),
-        name="answers",
-    )(lengths, state, own_map, arrived, next_map, table, probes, sources)
+        compiler_params=pltpu.CompilerParams(vmem_limit_bytes=CARRIED_MIB * MIB),
+        name="carried",
+    )(lengths, state, first[0], second[0], first[1], second[1], own, other, own_part, other_part, sources)
 
 
 def emit_kernel(local_ref, probe_ref, entry_ref, out_ref, rows_ref):
@@ -549,7 +633,7 @@
 
 def emit(local, probe, entry):
     heads, tokens, width = local.shape
-    rows = 2 * SPAN
+    rows = EMIT_ROWS
     spec = pl.BlockSpec((heads, rows, width), lambda c: (0, c, 0))
     return pl.pallas_call(
         emit_kernel,
@@ -558,25 +642,25 @@
         out_specs=pl.BlockSpec((rows, heads, width), lambda c: (c, 0, 0)),
         out_shape=jax.ShapeDtypeStruct((tokens, heads, width), BF16),
         scratch_shapes=[pltpu.VMEM((rows * heads, width), F32)],
-        compiler_params=pltpu.CompilerParams(vmem_limit_bytes=VMEM_BYTES),
+        compiler_params=pltpu.CompilerParams(vmem_limit_bytes=EMIT_BYTES),
         cost_estimate=pl.CostEstimate(flops=10**9, bytes_accessed=8 * MIB, transcendentals=0),
         name="emit",
     )(local, probe, entry)
 
 
-def finish_kernel(live, mine_ref, theirs_ref, local_ref, out_ref, rows_ref):
+def finish_kernel(live, mine_ref, near_ref, far_ref, local_ref, out_ref, rows_ref):
     slots, steps, heads, width = out_ref.shape
     for h in range(heads):
-        rows_ref[pl.ds(h, steps * slots, stride=heads), :] = mine_ref[h].astype(F32) + theirs_ref[
-            h
-        ].astype(F32)
+        rows_ref[pl.ds(h, steps * slots, stride=heads), :] = (
+            mine_ref[0, h].astype(F32) + near_ref[0, h].astype(F32)
+        ) + far_ref[0, h].astype(F32)
     on = iota2((slots, heads, width), 0) < live[0]
     for t in range(steps):
         part = rows_ref[pl.ds(t * slots * heads, slots * heads), :].reshape(slots, heads, width)
         out_ref[:, t] = jnp.where(on, part + local_ref[t], 0.0).astype(BF16)
 
 
-def finish(live, mine, theirs, local):
+def finish(live, mine, near, far, local):
     steps, slots, heads, width = local.shape
     return pl.pallas_call(
         finish_kernel,
@@ -584,17 +668,18 @@
             num_scalar_prefetch=1,
             grid=(1,),
             in_specs=[
-                pl.BlockSpec(mine.shape, lambda i, s: (0, 0, 0)),
-                pl.BlockSpec(mine.shape, lambda i, s: (0, 0, 0)),
+                pl.BlockSpec((1,) + mine.shape[1:], lambda i, s: (0, 0, 0, 0)),
+                pl.BlockSpec((1,) + near.shape[1:], lambda i, s: (0, 0, 0, 0)),
+                pl.BlockSpec((1,) + far.shape[1:], lambda i, s: (0, 0, 0, 0)),
                 pl.BlockSpec(local.shape, lambda i, s: (0, 0, 0, 0)),
             ],
             out_specs=pl.BlockSpec((slots, steps, heads, width), lambda i, s: (0, 0, 0, 0)),
             scratch_shapes=[pltpu.VMEM((steps * slots * heads, width), F32)],
         ),
         out_shape=jax.ShapeDtypeStruct((slots, steps, heads, width), BF16),
-        compiler_params=pltpu.CompilerParams(vmem_limit_bytes=VMEM_BYTES),
+        compiler_params=pltpu.CompilerParams(vmem_limit_bytes=SMALL_BYTES),
         name="finish",
-    )(live, mine, theirs, local)
+    )(live, mine, near, far, local)
 
 
 def shifted(array, by):
@@ -628,44 +713,70 @@
     longest = peers * spans // 2
     hops = max(1, (longest - 2) // spans + 1)
     probes, decode_local = requests(decode_query, decode_key, decode_value, decode_beta, decode_gate)
+    own_probes = [probes]
+    for x in range(1, peers):
+        pairs = [(i, i ^ reversed_bits(x, peers)) for i in range(peers)]
+        own_probes.append(lax.ppermute(probes, "dec", pairs))
     probes, prompt_key = lax.optimization_barrier((probes, prompt_key))
-    all_probes = lax.all_gather(probes, ("pre", "dec"), axis=0, tiled=False)
-    all_probes = all_probes.reshape((2, peers) + probes.shape)
     sources = request_source_prompt.reshape(2, peers, 1, -1)
     slots = sources.shape[3]
     sources = jnp.broadcast_to(sources, (2, peers, steps, slots)).reshape(2, peers, steps * slots, 1)
 
-    chunk_local, chunk_probe, state, sent, own_map, table = prefill(
+    chunk_local, chunk_probe, state, first, second, table = prefill(
         prompt_lengths, prompt_query[0], prompt_key[0], prompt_value[0], prompt_beta[0], prompt_gate[0]
     )
-    arrived = shifted(sent, 1) if hops > 1 else jnp.zeros_like(sent)
-    next_map = shifted(own_map, -1)
+    own_probes, first, second = lax.optimization_barrier((own_probes, first, second))
+    pairs = [(i, i ^ 1) for i in range(peers)]
+    first_got = lax.ppermute(first, "dec", pairs)
+    pairs = [(i, (i + 1 ^ 1) - 1) for i in range(1, peers - 1)]
+    second_got = lax.ppermute(second, "dec", pairs)
     if hops > 2:
+        odd = lax.axis_index("dec") % 2 == 1
         ends = jnp.cumsum(prompt_lengths[0]) - 1
         closed = jnp.any(ends // spans == lax.axis_index("dec"))
+        own_map = jnp.where(odd, first, second)
         through = jnp.where(closed, 0.0, own_map.astype(F32)).astype(BF16)
 
         def turn(_, arriving):
             leaving = state + jnp.einsum("hij,hjk->hik", through, arriving, preferred_element_type=F32)
             return shifted(leaving.astype(BF16), 1)
 
-        arrived = lax.fori_loop(0, hops - 2, turn, arrived)
-    leaving, keep, send = answers(
-        prompt_lengths, spans, state, own_map, arrived, next_map, table, all_probes, sources
+        arrived = lax.fori_loop(0, hops - 2, turn, jnp.where(odd, first_got, second_got))
+        first_got, second_got = (
+            jnp.where(odd, arrived, first_got),
+            jnp.where(odd, second_got, arrived),
+        )
+    own_probes = jnp.stack(own_probes)
+    other_probes = lax.ppermute(own_probes, "pre", [(0, 1), (1, 0)])
+    own_part, other_part = stored_answers(prompt_lengths, spans, table, own_probes, other_probes, sources)
+    leaving, keep, send = carried_answers(
+        prompt_lengths,
+        spans,
+        state,
+        (first, first_got),
+        (second, second_got),
+        own_probes,
+        other_probes,
+        own_part,
+        other_part,
+        sources,
     )
     theirs = lax.ppermute(send, "pre", [(0, 1), (1, 0)])
+    entry = shifted(leaving, 1)
     block = added(keep, theirs)
+    theirs = jnp.zeros_like(block)
     bit, part = 1, peers // 2
     while part:
         pairs = [(i, i ^ bit) for i in range(peers)]
-        theirs = lax.ppermute(block[part:], "dec", pairs)
-        block = block[:part]
         if bit == 1:
-            entry = shifted(leaving, 1)
-        if part > 1:
-            block = added(block, theirs)
+            outgoing = block[part:]
+        else:
+            outgoing = added(block[part : 2 * part], theirs[part : 2 * part])
+        if bit > 1 and part > 1:
+            block = added(block[:part], theirs[:part])
+        before, theirs = theirs, lax.ppermute(outgoing, "dec", pairs)
         bit, part = 2 * bit, part // 2
-    step_result = finish(live_counts, block[0], theirs[0], decode_local)
+    step_result = finish(live_counts, block, before, theirs, decode_local)
     prompt_result = emit(chunk_local, chunk_probe, entry)[None]
     return (prompt_result, step_result)
 

time: 96.5 us -> 67.2 us (0.70); the launches traced: 95 us -> 66.9 us
  between operations: 14.8 us -> 1.47 us
  Pallas kernels: 43.8 us -> 33.7 us
  starting transfers between devices: 12.2 us -> 17.8 us
  waiting for transfers between devices: 17.3 us -> 12.1 us
  local copies, waits for them, and re-layouts: 4.96 us -> 1.54 us
  other arithmetic: 2.02 us -> 0.29 us
    ppermute x2 -> x8, starting transfers between devices: 1.58 us -> 15.8 us  [the longest x2 8.56 us: local(): before, theirs = (theirs, lax.ppermute(outgoing, 'dec', pairs))]
    ppermute x3 -> x1, waiting for transfers between devices: 10.9 us -> 2.01 us  [shifted(): lax.ppermute(array, 'dec', [(i, i + by) for i in range(peers) if 0 <= i +...]
    ppermute x3 -> x1, starting transfers between devices: 9.65 us -> 1.93 us  [shifted(): lax.ppermute(array, 'dec', [(i, i + by) for i in range(peers) if 0 <= i +...]
    pallas_call x1, Pallas kernels: 7.37 us -> 2.64 us  [emit(): pl.pallas_call(emit_kernel, grid=(tokens // rows,), in_specs=[spec, spec,...]
    pallas_call x1 -> x2, Pallas kernels: 8.59 us -> 4.24 us  [the longest x1 2.93 us: stored_answers(): pl.pallas_call(functools.partial(stored_kernel, spans), grid_spec=pltpu.P...]
    ppermute x2 -> x8, waiting for transfers between devices: 4.63 us -> 8.16 us  [the longest x2 5.25 us: local(): before, theirs = (theirs, lax.ppermute(outgoing, 'dec', pairs))]
    broadcast_in_dim x1 -> x0, local copies, waits for them, and re-layouts: 1.24 us -> none  [requests(): jnp.transpose(jnp.stack([beta, gate]).astype(F32), (0, 2, 1, 3))[..., None]]
    convert_element_type x2, other arithmetic: 1.3 us -> 0.22 us  [added(): return (left.astype(F32) + right.astype(F32)).astype(BF16)]
  transfers between devices with their start and end apart: 7 -> 10, of which waited for: 5 -> 5; matrix products, arithmetic and copies ran while one was open for 2% -> 0% of each run, Pallas kernels for 32% -> 44%
where the time goes in v2:
time: 67.2 us; the launch traced here: 66.9 us
  Pallas kernels  33.7 us (50%)
  starting transfers between devices  17.8 us (26%)
  waiting for transfers between devices  12.1 us (18%)
  local copies, waits for them, and re-layouts  1.54 us (2%)
  between operations  1.47 us (2%)
    pallas_call x1, Pallas kernels, prefill(): pl.pallas_call(functools.partial(chunk_kernel, tokens // SPAN), grid_spec...  23.5 us
    ppermute x2, starting transfers between devices, local(): before, theirs = (theirs, lax.ppermute(outgoing, 'dec', pairs))  8.56 us
    ppermute x3, starting transfers between devices, local(): own_probes.append(lax.ppermute(probes, 'dec', pairs))  5.62 us
    ppermute x2, waiting for transfers between devices, local(): before, theirs = (theirs, lax.ppermute(outgoing, 'dec', pairs))  5.25 us
    pallas_call x1, Pallas kernels, stored_answers(): pl.pallas_call(functools.partial(stored_kernel, spans), grid_spec=pltpu.P...  2.93 us
    ppermute x1, waiting for transfers between devices, local(): first_got = lax.ppermute(first, 'dec', pairs)  2.87 us
    pallas_call x1, Pallas kernels, emit(): pl.pallas_call(emit_kernel, grid=(tokens // rows,), in_specs=[spec, spec,...  2.64 us
    pallas_call x1, Pallas kernels, requests(): pl.pallas_call(request_kernel, out_shape=[jax.ShapeDtypeStruct((heads, st...  2.56 us
  transfers between devices with their start and end apart: 10, of which 5 were waited for; matrix products, arithmetic and copies ran while one was open for 0% of the time, Pallas kernels for 44%

profile of v2, /device:TPU:0, one launch (start us, length us, event | category | flops | bytes accessed | tf_op | source)
XLA Modules:
  0.0 66.9 jit_solution(14802626701422020650)
XLA Ops:
  0.6 2.6 %requests.1 = (bf16[8,64,128]{2,1,0:T(8,128)(2,1)}, f32[4,16,8,128]{3,2,1,0:T(8,128)}) custom-call(bf16[16,4,8,128]{3,2,1,0:T(8,128)(2,1)} %q_ref.1, bf16[16,4,8,128]{3,2,1,0:T(8,128)(2,1)} %k_ref.1, bf16[16,4,8,128]{3,2,1,0:T(8,128)(2,1)} %v_ref.1, bf16[4,8,16]{2,1,0:T(8,128)(2,1)} %bitcast.17, bf16[4,8,16]{2,1,0:T(8,128)(2,1)} %bitcast.18), custom_call_target="tpu_custom_call" | custom-call | tf_op jit(solution)/shard_map/requests/pallas_call | solution.py:463
  3.2 4.0 %collective-permute-start = (bf16[8,64,128]{2,1,0:T(8,128)(2,1)}, bf16[8,64,128]{2,1,0:T(8,128)(2,1)S(1)}, u32[]{:S(2)}, u32[]{:S(2)}) collective-permute-start(bf16[8,64,128]{2,1,0:T(8,128)(2,1)} %get-tuple-element.31), channel_id=1, source_target_pairs={{0,8},{4,12},{8,0},{12,4},{1,9},{5,13},{9,1},{13,5},{2,10},{6,14},... | collective-permute-start | bytes 393224 | tf_op jit(solution)/shard_map/ppermute | solution.py:719
  7.2 1.6 %collective-permute-start.1 = (bf16[8,64,128]{2,1,0:T(8,128)(2,1)}, bf16[8,64,128]{2,1,0:T(8,128)(2,1)S(1)}, u32[]{:S(2)}, u32[]{:S(2)}) collective-permute-start(bf16[8,64,128]{2,1,0:T(8,128)(2,1)} %get-tuple-element.31), channel_id=1, source_target_pairs={{0,4},{4,0},{8,12},{12,8},{1,5},{5,1},{9,13},{13,9},{2,6},{6,2},{1... | collective-permute-start | bytes 393224 | tf_op jit(solution)/shard_map/ppermute | solution.py:719
  8.8 0.0 collective-permute-start.2
  8.8 23.5 %chunks.1 = (f32[8,1024,128]{2,1,0:T(8,128)}, bf16[8,1024,128]{2,1,0:T(8,128)(2,1)}, f32[8,128,128]{2,1,0:T(8,128)}, bf16[8,128,128]{2,1,0:T(8,128)(2,1)}, bf16[...) custom-call(s32[1,4]{1,0:T(1,128)} %lengths.5, bf16[1024,8,128]{2,1,0:T(8,128)(2,1)} %bitcast.19, ...), custom_call_target="tpu_custom_call" | custom-call | flops 6000000000 | bytes 16777216 | tf_op jit(solution)/shard_map/chunks/pallas_call | solution.py:389
  32.4 0.0 collective-permute-done
  32.4 0.0 collective-permute-done.1
  32.4 0.0 collective-permute-done.2
  32.4 0.1 pad_maximum_fusion.own_ref
  32.5 0.1 collective-permute-start.5
  32.6 0.9 %collective-permute-start.3 = (bf16[8,128,128]{2,1,0:T(8,128)(2,1)}, bf16[8,128,128]{2,1,0:T(8,128)(2,1)S(1)}, u32[]{:S(2)}, u32[]{:S(2)}) collective-permute-start(bf16[8,128,128]{2,1,0:T(8,128)(2,1)} %get-tuple-element.29.first_ref), channel_id=1, source_target_pairs={{0,4},{4,0},{8,12},{12,8},{1,5},{5,1},{9,13},{13,9},{2,6},{6,2},{1... | collective-permute-start | bytes 786440 | tf_op jit(solution)/shard_map/ppermute | solution.py:730
  33.5 0.7 collective-permute-start.4
  34.2 0.1 broadcast_in_dim.10
  34.3 0.2 reshape.10.source_ref
  34.5 0.0 collective-permute-done.5.other_ref
  34.5 1.2 %copy-done.7 = bf16[4,8,128,128]{3,2,1,0:T(8,128)(2,1)S(1)} copy-done((bf16[4,8,128,128]{3,2,1,0:T(8,128)(2,1)S(1)}, bf16[4,8,128,128]{3,2,1,0:T(8,128)(2,1)}, u32[]{:S(2)}) %copy-start.7) | copy-done | bytes 1048600
  35.7 2.9 %stored.1 = (bf16[4,8,64,128]{3,2,1,0:T(8,128)(2,1)S(1)}, bf16[4,8,64,128]{3,2,1,0:T(8,128)(2,1)S(1)}) custom-call(s32[1,4]{1,0:T(1,128)S(1)} %copy-done.6, bf16[4,8,128,128]{3,2,1,0:T(8,128)(2,1)S(1)} %copy-done.7, bf16[4,8,64,128]{3,2,1,0:T(8,128)(2,1)S(1)} %pad_maximum_fusion.own_ref, bf16[4,8,64,128]{3,2,1,0:T(8,128)(2,1)S(1)} %collective-permute-done.5.other_ref, ...), custom_call_target="tpu_custom_call" | custom-call | flops 1000000000 | bytes 16777216 | tf_op jit(solution)/shard_map/stored/pallas_call | solution.py:535
  38.7 2.9 %collective-permute-done.3.first_got_ref = bf16[8,128,128]{2,1,0:T(8,128)(2,1)S(1)} collective-permute-done((bf16[8,128,128]{2,1,0:T(8,128)(2,1)}, bf16[8,128,128]{2,1,0:T(8,128)(2,1)S(1)}, u32[]{:S(2)}, u32[]{:S(2)}) %collective-permute-start.3) | collective-permute-done | bytes 262176 | tf_op jit(solution)/shard_map/ppermute | solution.py:730
  41.5 0.0 collective-permute-done.4.second_got_ref
  41.6 1.3 %carried.1 = (bf16[8,128,128]{2,1,0:T(8,128)(2,1)S(1)}, bf16[4,8,64,128]{3,2,1,0:T(8,128)(2,1)S(1)}, bf16[4,8,64,128]{3,2,1,0:T(8,128)(2,1)S(1)}) custom-call(s32[1,4]{1,0:T(1,128)S(1)} %copy-done.6, f32[8,128,128]{2,1,0:T(8,128)S(1)} %copy-done.2, bf16[8,128,128]{2,1,0:T(8,128)(2,1)S(1)} %copy-done.4, bf16[8,128,128]{2,1,0:T(8,128)(2,1)S(1)} %copy-done.5, ...), custom_call_target="tpu_custom_call" | custom-call | tf_op jit(solution)/shard_map/carried/pallas_call | solution.py:612
  42.9 0.0 copy-start.1
  42.9 0.1 collective-permute-start.7
  43.0 1.9 %collective-permute-done.7 = bf16[4,8,64,128]{3,2,1,0:T(8,128)(2,1)S(1)} collective-permute-done((bf16[4,8,64,128]{3,2,1,0:T(8,128)(2,1)S(1)}, bf16[4,8,64,128]{3,2,1,0:T(8,128)(2,1)S(1)}, u32[]{:S(2)}, u32[]{:S(2)}) %collective-permute-start.7) | collective-permute-done | bytes 524320 | tf_op jit(solution)/shard_map/ppermute | solution.py:764
  44.9 0.2 add_convert_fusion.mine_ref
  45.1 5.6 %collective-permute-start.8 = (bf16[2,8,64,128]{3,2,1,0:T(8,128)(2,1)S(1)}, bf16[2,8,64,128]{3,2,1,0:T(8,128)(2,1)S(1)}, u32[]{:S(2)}, u32[]{:S(2)}) collective-permute-start(bf16[2,8,64,128]{3,2,1,0:T(8,128)(2,1)S(1)} %slice.12), channel_id=1, source_target_pairs={{0,4},{4,0},{8,12},{12,8},{1,5},{5,1},{9,13},{13,9},{2,6},{6,2},{1... | collective-permute-start | bytes 786440 | tf_op jit(solution)/shard_map/ppermute | solution.py:777
  50.7 1.9 %collective-permute-start.6 = (bf16[8,128,128]{2,1,0:T(8,128)(2,1)S(1)}, bf16[8,128,128]{2,1,0:T(8,128)(2,1)S(1)}, u32[]{:S(2)}, u32[]{:S(2)}) collective-permute-start(bf16[8,128,128]{2,1,0:T(8,128)(2,1)S(1)} %get-tuple-element.38), channel_id=1, source_target_pairs={{0,4},{4,8},{8,12},{1,5},{5,9},{9,13},{2,6},{6,10},{10,14},{3,7},{... | collective-permute-start | bytes 786440 | tf_op jit(solution)/shard_map/ppermute | solution.py:687
  52.7 4.7 %collective-permute-done.8.near_ref = bf16[2,8,64,128]{3,2,1,0:T(8,128)(2,1)S(1)} collective-permute-done((bf16[2,8,64,128]{3,2,1,0:T(8,128)(2,1)S(1)}, bf16[2,8,64,128]{3,2,1,0:T(8,128)(2,1)S(1)}, u32[]{:S(2)}, u32[]{:S(2)}) %collective-permute-start.8) | collective-permute-done | bytes 262176 | tf_op jit(solution)/shard_map/ppermute | solution.py:777
  57.4 2.9 %collective-permute-start.9 = (bf16[1,8,64,128]{3,2,1,0:T(8,128)(2,1)S(1)}, bf16[1,8,64,128]{3,2,1,0:T(8,128)(2,1)S(1)}, u32[]{:S(2)}, u32[]{:S(2)}) collective-permute-start(bf16[1,8,64,128]{3,2,1,0:T(8,128)(2,1)S(1)} %add_convert_fusion.1), channel_id=1, source_target_pairs={{0,8},{4,12},{8,0},{12,4},{1,9},{5,13},{9,1},{13,5},{2,10},{6,14},... | collective-permute-start | bytes 393224 | tf_op jit(solution)/shard_map/ppermute | solution.py:777
  61.0 2.0 %collective-permute-done.6.entry_ref = bf16[8,128,128]{2,1,0:T(8,128)(2,1)S(1)} collective-permute-done((bf16[8,128,128]{2,1,0:T(8,128)(2,1)S(1)}, bf16[8,128,128]{2,1,0:T(8,128)(2,1)S(1)}, u32[]{:S(2)}, u32[]{:S(2)}) %collective-permute-start.6) | collective-permute-done | bytes 262176 | tf_op jit(solution)/shard_map/ppermute | solution.py:687
  63.0 2.6 %emit.1 = bf16[1024,8,128]{2,1,0:T(8,128)(2,1)} custom-call(f32[8,1024,128]{2,1,0:T(8,128)S(1)} %copy-done, bf16[8,1024,128]{2,1,0:T(8,128)(2,1)S(1)} %copy-done.1, bf16[8,128,128]{2,1,0:T(8,128)(2,1)S(1)} %collective-permute-done.6.entry_ref), custom_call_target="tpu_custom_call" | custom-call | flops 1000000000 | bytes 8388608 | tf_op jit(solution)/shard_map/emit/pallas_call | solution.py:638
  65.7 0.5 collective-permute-done.9.far_ref
  66.2 0.8 %finish.1 = bf16[16,4,8,128]{3,2,1,0:T(8,128)(2,1)} custom-call(s32[1]{0:T(128)S(6)} %copy.17.live, bf16[4,8,64,128]{3,2,1,0:T(8,128)(2,1)S(1)} %add_convert_fusion.mine_ref, bf16[2,8,64,128]{3,2,1,0:T(8,128)(2,1)S(1)} %collective-permute-done.8.near_ref, bf16[1,8,64,128]{3,2,1,0:T(8,128)(2,1)S(1)} %collective-permute-done.9.far_ref, ...), custom_call_target="tpu_custom_call" | custom-call | tf_op jit(solution)/shard_map/finish/pallas_call | solution.py:665
  (21 shorter events, 0.1 us)
Async XLA Ops:
  3.2 29.2 %collective-permute-start = (bf16[8,64,128]{2,1,0:T(8,128)(2,1)}, bf16[8,64,128]{2,1,0:T(8,128)(2,1)S(1)}, u32[]{:S(2)}, u32[]{:S(2)}) collective-permute-start(bf16[8,64,128]{2,1,0:T(8,128)(2,1)} %get-tuple-element.31), channel_id=1, source_target_pairs={{0,8},{4,12},{8,0},{12,4},{1,9},{5,13},{9,1},{13,5},{2,10},{6,14},... | collective-permute-start | bytes 393224 | tf_op jit(solution)/shard_map/ppermute | solution.py:719
  7.2 25.2 %collective-permute-start.1 = (bf16[8,64,128]{2,1,0:T(8,128)(2,1)}, bf16[8,64,128]{2,1,0:T(8,128)(2,1)S(1)}, u32[]{:S(2)}, u32[]{:S(2)}) collective-permute-start(bf16[8,64,128]{2,1,0:T(8,128)(2,1)} %get-tuple-element.31), channel_id=1, source_target_pairs={{0,4},{4,0},{8,12},{12,8},{1,5},{5,1},{9,13},{13,9},{2,6},{6,2},{1... | collective-permute-start | bytes 393224 | tf_op jit(solution)/shard_map/ppermute | solution.py:719
  8.8 23.6 %collective-permute-start.2 = (bf16[8,64,128]{2,1,0:T(8,128)(2,1)}, bf16[8,64,128]{2,1,0:T(8,128)(2,1)S(1)}, u32[]{:S(2)}, u32[]{:S(2)}) collective-permute-start(bf16[8,64,128]{2,1,0:T(8,128)(2,1)} %get-tuple-element.31), channel_id=1, source_target_pairs={{0,12},{4,8},{8,4},{12,0},{1,13},{5,9},{9,5},{13,1},{2,14},{6,10},... | collective-permute-start | bytes 393224 | tf_op jit(solution)/shard_map/ppermute | solution.py:719
  8.8 23.6 %copy-start.8 = (bf16[8,64,128]{2,1,0:T(8,128)(2,1)S(1)}, bf16[8,64,128]{2,1,0:T(8,128)(2,1)}, u32[]{:S(2)}) copy-start(bf16[8,64,128]{2,1,0:T(8,128)(2,1)} %get-tuple-element.31) | copy-start | bytes 393220
  8.8 25.4 %copy-start.9 = (s32[128]{0:T(128)S(1)}, s32[128]{0:T(128)}, u32[]{:S(2)}) copy-start(s32[128]{0:T(128)} %param.19) | copy-start | bytes 1540
  8.8 25.7 %copy-start.6 = (s32[1,4]{1,0:T(1,128)S(1)}, s32[1,4]{1,0:T(1,128)}, u32[]{:S(2)}) copy-start(s32[1,4]{1,0:T(1,128)} %lengths.5) | copy-start | bytes 52
  32.5 9.0 %copy-start.2 = (f32[8,128,128]{2,1,0:T(8,128)S(1)}, f32[8,128,128]{2,1,0:T(8,128)}, u32[]{:S(2)}) copy-start(f32[8,128,128]{2,1,0:T(8,128)} %get-tuple-element.26.state_ref) | copy-start | bytes 1572868
  32.5 9.0 %copy-start.4 = (bf16[8,128,128]{2,1,0:T(8,128)(2,1)S(1)}, bf16[8,128,128]{2,1,0:T(8,128)(2,1)}, u32[]{:S(2)}) copy-start(bf16[8,128,128]{2,1,0:T(8,128)(2,1)} %get-tuple-element.29.first_ref) | copy-start | bytes 786436
  32.5 9.0 %copy-start.5 = (bf16[8,128,128]{2,1,0:T(8,128)(2,1)S(1)}, bf16[8,128,128]{2,1,0:T(8,128)(2,1)}, u32[]{:S(2)}) copy-start(bf16[8,128,128]{2,1,0:T(8,128)(2,1)} %get-tuple-element.30.second_ref) | copy-start | bytes 786436
  32.5 2.0 %collective-permute-start.5 = (bf16[4,8,64,128]{3,2,1,0:T(8,128)(2,1)S(1)}, bf16[4,8,64,128]{3,2,1,0:T(8,128)(2,1)S(1)}, u32[]{:S(2)}, u32[]{:S(2)}) collective-permute-start(bf16[4,8,64,128]{3,2,1,0:T(8,128)(2,1)S(1)} %pad_maximum_fusion.own_ref), channel_id=1, source_target_pairs={{0,16},{16,0},{1,17},{17,1},{2,18},{18,2},{3,19},{19,3},{4,20},{20... | collective-permute-start | bytes 1572872 | tf_op jit(solution)/shard_map/ppermute | solution.py:750
  32.6 8.9 %collective-permute-start.3 = (bf16[8,128,128]{2,1,0:T(8,128)(2,1)}, bf16[8,128,128]{2,1,0:T(8,128)(2,1)S(1)}, u32[]{:S(2)}, u32[]{:S(2)}) collective-permute-start(bf16[8,128,128]{2,1,0:T(8,128)(2,1)} %get-tuple-element.29.first_ref), channel_id=1, source_target_pairs={{0,4},{4,0},{8,12},{12,8},{1,5},{5,1},{9,13},{13,9},{2,6},{6,2},{1... | collective-permute-start | bytes 786440 | tf_op jit(solution)/shard_map/ppermute | solution.py:730
  33.5 8.0 %collective-permute-start.4 = (bf16[8,128,128]{2,1,0:T(8,128)(2,1)}, bf16[8,128,128]{2,1,0:T(8,128)(2,1)S(1)}, u32[]{:S(2)}, u32[]{:S(2)}) collective-permute-start(bf16[8,128,128]{2,1,0:T(8,128)(2,1)} %get-tuple-element.30.second_ref), channel_id=1, source_target_pairs={{4,8},{8,4},{5,9},{9,5},{6,10},{10,6},{7,11},{11,7},{20,24},{24,20... | collective-permute-start | bytes 786440 | tf_op jit(solution)/shard_map/ppermute | solution.py:732
  34.5 1.2 %copy-start.7 = (bf16[4,8,128,128]{3,2,1,0:T(8,128)(2,1)S(1)}, bf16[4,8,128,128]{3,2,1,0:T(8,128)(2,1)}, u32[]{:S(2)}) copy-start(bf16[4,8,128,128]{3,2,1,0:T(8,128)(2,1)} %get-tuple-element.35.table_ref) | copy-start | bytes 3145732
  41.6 21.5 %copy-start = (f32[8,1024,128]{2,1,0:T(8,128)S(1)}, f32[8,1024,128]{2,1,0:T(8,128)}, u32[]{:S(2)}) copy-start(f32[8,1024,128]{2,1,0:T(8,128)} %get-tuple-element.24.local_ref) | copy-start | bytes 12582916
  42.9 20.1 %copy-start.1 = (bf16[8,1024,128]{2,1,0:T(8,128)(2,1)S(1)}, bf16[8,1024,128]{2,1,0:T(8,128)(2,1)}, u32[]{:S(2)}) copy-start(bf16[8,1024,128]{2,1,0:T(8,128)(2,1)} %get-tuple-element.25.probe_ref) | copy-start | bytes 6291460
  42.9 2.0 %collective-permute-start.7 = (bf16[4,8,64,128]{3,2,1,0:T(8,128)(2,1)S(1)}, bf16[4,8,64,128]{3,2,1,0:T(8,128)(2,1)S(1)}, u32[]{:S(2)}, u32[]{:S(2)}) collective-permute-start(bf16[4,8,64,128]{3,2,1,0:T(8,128)(2,1)S(1)} %get-tuple-element.40), channel_id=1, source_target_pairs={{0,16},{16,0},{1,17},{17,1},{2,18},{18,2},{3,19},{19,3},{4,20},{20... | collective-permute-start | bytes 1572872 | tf_op jit(solution)/shard_map/ppermute | solution.py:764
  45.1 12.3 %collective-permute-start.8 = (bf16[2,8,64,128]{3,2,1,0:T(8,128)(2,1)S(1)}, bf16[2,8,64,128]{3,2,1,0:T(8,128)(2,1)S(1)}, u32[]{:S(2)}, u32[]{:S(2)}) collective-permute-start(bf16[2,8,64,128]{3,2,1,0:T(8,128)(2,1)S(1)} %slice.12), channel_id=1, source_target_pairs={{0,4},{4,0},{8,12},{12,8},{1,5},{5,1},{9,13},{13,9},{2,6},{6,2},{1... | collective-permute-start | bytes 786440 | tf_op jit(solution)/shard_map/ppermute | solution.py:777
  50.7 12.3 %collective-permute-start.6 = (bf16[8,128,128]{2,1,0:T(8,128)(2,1)S(1)}, bf16[8,128,128]{2,1,0:T(8,128)(2,1)S(1)}, u32[]{:S(2)}, u32[]{:S(2)}) collective-permute-start(bf16[8,128,128]{2,1,0:T(8,128)(2,1)S(1)} %get-tuple-element.38), channel_id=1, source_target_pairs={{0,4},{4,8},{8,12},{1,5},{5,9},{9,13},{2,6},{6,10},{10,14},{3,7},{... | collective-permute-start | bytes 786440 | tf_op jit(solution)/shard_map/ppermute | solution.py:687
  57.4 8.7 %collective-permute-start.9 = (bf16[1,8,64,128]{3,2,1,0:T(8,128)(2,1)S(1)}, bf16[1,8,64,128]{3,2,1,0:T(8,128)(2,1)S(1)}, u32[]{:S(2)}, u32[]{:S(2)}) collective-permute-start(bf16[1,8,64,128]{3,2,1,0:T(8,128)(2,1)S(1)} %add_convert_fusion.1), channel_id=1, source_target_pairs={{0,8},{4,12},{8,0},{12,4},{1,9},{5,13},{9,1},{13,5},{2,10},{6,14},... | collective-permute-start | bytes 393224 | tf_op jit(solution)/shard_map/ppermute | solution.py:777
  63.0 3.2 %copy-start.3 = (f32[4,16,8,128]{3,2,1,0:T(8,128)S(1)}, f32[4,16,8,128]{3,2,1,0:T(8,128)}, u32[]{:S(2)}) copy-start(f32[4,16,8,128]{3,2,1,0:T(8,128)} %get-tuple-element.41.local_ref) | copy-start | bytes 786436

commit v3 on v2

--- a/solution.py
+++ b/solution.py
@@ -418,57 +418,62 @@
     )(lengths, query, key, value, beta, gate)
 
 
-def request_kernel(q_ref, k_ref, v_ref, beta_ref, gate_ref, probe_ref, local_ref, rows_ref):
+def per_slot(ref, t, slots, heads, width):
+    values = ref[t].astype(F32)
+    return jnp.stack([jnp.broadcast_to(values[:, i : i + 1], (heads, width)) for i in range(slots)])
+
+
+def request_kernel(probing, q_ref, k_ref, v_ref, beta_ref, gate_ref, out_ref, *scratch):
     slots, steps, heads, width = q_ref.shape
-
-    def per_slot(ref, t):
-        values = ref[t].astype(F32)
-        return jnp.stack(
-            [jnp.broadcast_to(values[:, i : i + 1], (heads, width)) for i in range(slots)]
-        )
-
     keys = [unit(k_ref[:, t].astype(F32)) for t in range(steps)]
     queries = [unit(q_ref[:, t].astype(F32)) for t in range(steps)]
-    gates = []
+    gates, sources = [], []
     for t in range(steps):
-        gate = per_slot(gate_ref, t)
+        gate = per_slot(gate_ref, t, slots, heads, width)
         gates.append(gate if t == 0 else gates[-1] + gate)
-    weights, updates = [], []
     for t in range(steps):
-        beta = per_slot(beta_ref, t)
-        reach = jnp.exp(gates[t]) * keys[t]
-        value = v_ref[:, t].astype(F32)
+        beta = per_slot(beta_ref, t, slots, heads, width)
+        source = jnp.exp(gates[t]) * keys[t] if probing else v_ref[:, t].astype(F32)
         for s in range(t):
             factor = jnp.exp(gates[t] - gates[s]) * jnp.sum(keys[s] * keys[t], axis=-1, keepdims=True)
-            reach = reach - factor * weights[s]
-            value = value - factor * updates[s]
-        weights.append(beta * reach)
-        updates.append(beta * value)
-        probe = jnp.exp(gates[t]) * queries[t]
-        emitted = jnp.zeros_like(value)
+            source = source - factor * sources[s]
+        sources.append(beta * source)
+        result = jnp.exp(gates[t]) * queries[t] if probing else jnp.zeros_like(source)
         for s in range(t + 1):
             factor = jnp.sum(keys[s] * queries[t], axis=-1, keepdims=True)
             factor = factor if s == t else factor * jnp.exp(gates[t] - gates[s])
-            probe = probe - factor * weights[s]
-            emitted = emitted + factor * updates[s]
-        rows_ref[pl.ds(t * slots * heads, slots * heads), :] = probe.reshape(slots * heads, width)
-        local_ref[t] = emitted
-    for h in range(heads):
-        probe_ref[h] = rows_ref[pl.ds(h, steps * slots, stride=heads), :].astype(BF16)
-
-
-def requests(query, key, value, beta, gate):
+            result = result - factor * sources[s] if probing else result + factor * sources[s]
+        if probing:
+            scratch[0][pl.ds(t * slots * heads, slots * heads), :] = result.reshape(slots * heads, width)
+        else:
+            out_ref[t] = result
+    if probing:
+        for h in range(heads):
+            out_ref[h] = scratch[0][pl.ds(h, steps * slots, stride=heads), :].astype(BF16)
+
+
+def probe_kernel(q_ref, k_ref, beta_ref, gate_ref, out_ref, rows_ref):
+    request_kernel(True, q_ref, k_ref, None, beta_ref, gate_ref, out_ref, rows_ref)
+
+
+def request_probes(query, key, beta, gate):
     slots, steps, heads, width = query.shape
-    beta, gate = jnp.transpose(beta, (1, 2, 0)), jnp.transpose(gate, (1, 2, 0))
     return pl.pallas_call(
-        request_kernel,
-        out_shape=[
-            jax.ShapeDtypeStruct((heads, steps * slots, width), BF16),
-            jax.ShapeDtypeStruct((steps, slots, heads, width), F32),
-        ],
+        probe_kernel,
+        out_shape=jax.ShapeDtypeStruct((heads, steps * slots, width), BF16),
         scratch_shapes=[pltpu.VMEM((steps * slots * heads, width), F32)],
         compiler_params=pltpu.CompilerParams(vmem_limit_bytes=VMEM_BYTES),
-        name="requests",
+        name="probes",
+    )(query, key, beta, gate)
+
+
+def request_locals(query, key, value, beta, gate):
+    slots, steps, heads, width = query.shape
+    return pl.pallas_call(
+        functools.partial(request_kernel, False),
+        out_shape=jax.ShapeDtypeStruct((steps, slots, heads, width), F32),
+        compiler_params=pltpu.CompilerParams(vmem_limit_bytes=SMALL_BYTES),
+        name="locals",
     )(query, key, value, beta, gate)
 
 
@@ -712,7 +717,9 @@
     steps = decode_query.shape[1]
     longest = peers * spans // 2
     hops = max(1, (longest - 2) // spans + 1)
-    probes, decode_local = requests(decode_query, decode_key, decode_value, decode_beta, decode_gate)
+    step_beta = jnp.transpose(decode_beta, (1, 2, 0))
+    step_gate = jnp.transpose(decode_gate, (1, 2, 0))
+    probes = request_probes(decode_query, decode_key, step_beta, step_gate)
     own_probes = [probes]
     for x in range(1, peers):
         pairs = [(i, i ^ reversed_bits(x, peers)) for i in range(peers)]
@@ -725,7 +732,10 @@
     chunk_local, chunk_probe, state, first, second, table = prefill(
         prompt_lengths, prompt_query[0], prompt_key[0], prompt_value[0], prompt_beta[0], prompt_gate[0]
     )
-    own_probes, first, second = lax.optimization_barrier((own_probes, first, second))
+    own_probes, first, second, decode_value = lax.optimization_barrier(
+        (own_probes, first, second, decode_value)
+    )
+    decode_local = request_locals(decode_query, decode_key, decode_value, step_beta, step_gate)
     pairs = [(i, i ^ 1) for i in range(peers)]
     first_got = lax.ppermute(first, "dec", pairs)
     pairs = [(i, (i + 1 ^ 1) - 1) for i in range(1, peers - 1)]

time: 67.2 us -> 66.4 us (0.988)
  Pallas kernels: 33.7 us -> 33 us
    pallas_call x1, Pallas kernels: 2.93 us -> 1.7 us  [stored_answers(): pl.pallas_call(functools.partial(stored_kernel, spans), grid_spec=pltpu.P...]
    ppermute x1, starting transfers between devices: 0.91 us -> 1.79 us  [local(): first_got = lax.ppermute(first, 'dec', pairs)]
    ppermute x2, starting transfers between devices: 8.56 us -> 7.79 us  [local(): before, theirs = (theirs, lax.ppermute(outgoing, 'dec', pairs))]
    pallas_call x1 -> x2, Pallas kernels: 2.56 us -> 3.05 us  [the longest x1 2.36 us: request_probes(): pl.pallas_call(probe_kernel, out_shape=jax.ShapeDtypeStruct((heads, steps...]
  transfers between devices with their start and end apart: 10 -> 10, of which waited for: 5 -> 5; matrix products, arithmetic and copies ran while one was open for 0% -> 0% of each run, Pallas kernels for 44% -> 43%
where the time goes in v3:
time: 66.4 us; the launch traced here: 66.3 us
  Pallas kernels  33 us (50%)
  starting transfers between devices  18 us (27%)
  waiting for transfers between devices  12 us (18%)
  local copies, waits for them, and re-layouts  1.55 us (2%)
  between operations  1.55 us (2%)
    pallas_call x1, Pallas kernels, prefill(): pl.pallas_call(functools.partial(chunk_kernel, tokens // SPAN), grid_spec...  23.5 us
    ppermute x2, starting transfers between devices, local(): before, theirs = (theirs, lax.ppermute(outgoing, 'dec', pairs))  7.79 us
    ppermute x3, starting transfers between devices, local(): own_probes.append(lax.ppermute(probes, 'dec', pairs))  5.62 us
    ppermute x2, waiting for transfers between devices, local(): before, theirs = (theirs, lax.ppermute(outgoing, 'dec', pairs))  5.26 us
    ppermute x1, waiting for transfers between devices, local(): first_got = lax.ppermute(first, 'dec', pairs)  3.19 us
    pallas_call x1, Pallas kernels, emit(): pl.pallas_call(emit_kernel, grid=(tokens // rows,), in_specs=[spec, spec,...  2.63 us
    pallas_call x1, Pallas kernels, request_probes(): pl.pallas_call(probe_kernel, out_shape=jax.ShapeDtypeStruct((heads, steps...  2.36 us
    ppermute x1, starting transfers between devices, shifted(): lax.ppermute(array, 'dec', [(i, i + by) for i in range(peers) if 0 <= i +...  1.93 us
  transfers between devices with their start and end apart: 10, of which 5 were waited for; matrix products, arithmetic and copies ran while one was open for 0% of the time, Pallas kernels for 43%

profile of v3, /device:TPU:0, one launch (start us, length us, event | category | flops | bytes accessed | tf_op | source)
XLA Modules:
  0.0 66.3 jit_solution(11707960356587912567)
XLA Ops:
  0.6 2.4 %probes.1 = bf16[8,64,128]{2,1,0:T(8,128)(2,1)} custom-call(bf16[16,4,8,128]{3,2,1,0:T(8,128)(2,1)} %q_ref.3, bf16[16,4,8,128]{3,2,1,0:T(8,128)(2,1)} %k_ref.3, bf16[4,8,16]{2,1,0:T(8,128)(2,1)} %bitcast.12, bf16[4,8,16]{2,1,0:T(8,128)(2,1)} %bitcast.14), custom_call_target="tpu_custom_call" | custom-call | tf_op jit(solution)/shard_map/probes/pallas_call | solution.py:461
  3.0 4.0 %collective-permute-start = (bf16[8,64,128]{2,1,0:T(8,128)(2,1)}, bf16[8,64,128]{2,1,0:T(8,128)(2,1)S(1)}, u32[]{:S(2)}, u32[]{:S(2)}) collective-permute-start(bf16[8,64,128]{2,1,0:T(8,128)(2,1)} %probes.1), channel_id=1, source_target_pairs={{0,8},{4,12},{8,0},{12,4},{1,9},{5,13},{9,1},{13,5},{2,10},{6,14},... | collective-permute-start | bytes 393224 | tf_op jit(solution)/shard_map/ppermute | solution.py:726
  7.0 1.6 %collective-permute-start.1 = (bf16[8,64,128]{2,1,0:T(8,128)(2,1)}, bf16[8,64,128]{2,1,0:T(8,128)(2,1)S(1)}, u32[]{:S(2)}, u32[]{:S(2)}) collective-permute-start(bf16[8,64,128]{2,1,0:T(8,128)(2,1)} %probes.1), channel_id=1, source_target_pairs={{0,4},{4,0},{8,12},{12,8},{1,5},{5,1},{9,13},{13,9},{2,6},{6,2},{1... | collective-permute-start | bytes 393224 | tf_op jit(solution)/shard_map/ppermute | solution.py:726
  8.6 23.5 %chunks.1 = (f32[8,1024,128]{2,1,0:T(8,128)}, bf16[8,1024,128]{2,1,0:T(8,128)(2,1)}, f32[8,128,128]{2,1,0:T(8,128)}, bf16[8,128,128]{2,1,0:T(8,128)(2,1)}, bf16[...) custom-call(s32[1,4]{1,0:T(1,128)} %lengths.5, bf16[1024,8,128]{2,1,0:T(8,128)(2,1)} %bitcast.21, ...), custom_call_target="tpu_custom_call" | custom-call | flops 6000000000 | bytes 16777216 | tf_op jit(solution)/shard_map/chunks/pallas_call | solution.py:389
  32.2 0.0 collective-permute-done.1
  32.2 0.0 collective-permute-done.2
  32.2 0.1 pad_maximum_fusion.own_ref
  32.3 0.1 collective-permute-start.5
  32.4 1.8 %collective-permute-start.3 = (bf16[8,128,128]{2,1,0:T(8,128)(2,1)}, bf16[8,128,128]{2,1,0:T(8,128)(2,1)S(1)}, u32[]{:S(2)}, u32[]{:S(2)}) collective-permute-start(bf16[8,128,128]{2,1,0:T(8,128)(2,1)} %get-tuple-element.27.first_ref), channel_id=1, source_target_pairs={{0,4},{4,0},{8,12},{12,8},{1,5},{5,1},{9,13},{13,9},{2,6},{6,2},{1... | collective-permute-start | bytes 786440 | tf_op jit(solution)/shard_map/ppermute | solution.py:740
  34.2 0.7 %collective-permute-start.4 = (bf16[8,128,128]{2,1,0:T(8,128)(2,1)}, bf16[8,128,128]{2,1,0:T(8,128)(2,1)S(1)}, u32[]{:S(2)}, u32[]{:S(2)}) collective-permute-start(bf16[8,128,128]{2,1,0:T(8,128)(2,1)} %get-tuple-element.28.second_ref), channel_id=1, source_target_pairs={{4,8},{8,4},{5,9},{9,5},{6,10},{10,6},{7,11},{11,7},{20,24},{24,20... | collective-permute-start | bytes 786440 | tf_op jit(solution)/shard_map/ppermute | solution.py:742
  34.9 0.1 broadcast_in_dim.10
  35.0 0.2 reshape.10.source_ref
  35.2 0.0 collective-permute-done.5.other_ref
  35.2 1.2 %copy-done.11 = bf16[4,8,128,128]{3,2,1,0:T(8,128)(2,1)S(1)} copy-done((bf16[4,8,128,128]{3,2,1,0:T(8,128)(2,1)S(1)}, bf16[4,8,128,128]{3,2,1,0:T(8,128)(2,1)}, u32[]{:S(2)}) %copy-start.11) | copy-done | bytes 1048600
  36.4 1.7 %stored.1 = (bf16[4,8,64,128]{3,2,1,0:T(8,128)(2,1)S(1)}, bf16[4,8,64,128]{3,2,1,0:T(8,128)(2,1)S(1)}) custom-call(s32[1,4]{1,0:T(1,128)S(1)} %copy-done.10, bf16[4,8,128,128]{3,2,1,0:T(8,128)(2,1)S(1)} %copy-done.11, bf16[4,8,64,128]{3,2,1,0:T(8,128)(2,1)S(1)} %pad_maximum_fusion.own_ref, bf16[4,8,64,128]{3,2,1,0:T(8,128)(2,1)S(1)} %collective-permute-done.5.other_ref, ...), custom_call_target="tpu_custom_call" | custom-call | flops 1000000000 | bytes 16777216 | tf_op jit(solution)/shard_map/stored/pallas_call | solution.py:540
  38.1 3.2 %collective-permute-done.3.first_got_ref = bf16[8,128,128]{2,1,0:T(8,128)(2,1)S(1)} collective-permute-done((bf16[8,128,128]{2,1,0:T(8,128)(2,1)}, bf16[8,128,128]{2,1,0:T(8,128)(2,1)S(1)}, u32[]{:S(2)}, u32[]{:S(2)}) %collective-permute-start.3) | collective-permute-done | bytes 262176 | tf_op jit(solution)/shard_map/ppermute | solution.py:740
  41.4 1.3 %carried.1 = (bf16[8,128,128]{2,1,0:T(8,128)(2,1)S(1)}, bf16[4,8,64,128]{3,2,1,0:T(8,128)(2,1)S(1)}, bf16[4,8,64,128]{3,2,1,0:T(8,128)(2,1)S(1)}) custom-call(s32[1,4]{1,0:T(1,128)S(1)} %copy-done.10, f32[8,128,128]{2,1,0:T(8,128)S(1)} %copy-done.2, bf16[8,128,128]{2,1,0:T(8,128)(2,1)S(1)} %copy-done.5, bf16[8,128,128]{2,1,0:T(8,128)(2,1)S(1)} %copy-done.6, ...), custom_call_target="tpu_custom_call" | custom-call | tf_op jit(solution)/shard_map/carried/pallas_call | solution.py:617
  42.7 0.0 copy-start.3
  42.7 0.0 copy-start.8
  42.7 0.0 copy-start.1
  42.7 0.1 collective-permute-start.7
  42.8 1.9 %collective-permute-done.7 = bf16[4,8,64,128]{3,2,1,0:T(8,128)(2,1)S(1)} collective-permute-done((bf16[4,8,64,128]{3,2,1,0:T(8,128)(2,1)S(1)}, bf16[4,8,64,128]{3,2,1,0:T(8,128)(2,1)S(1)}, u32[]{:S(2)}, u32[]{:S(2)}) %collective-permute-start.7) | collective-permute-done | bytes 524320 | tf_op jit(solution)/shard_map/ppermute | solution.py:774
  44.7 0.2 add_convert_fusion.mine_ref
  44.9 5.2 %collective-permute-start.8 = (bf16[2,8,64,128]{3,2,1,0:T(8,128)(2,1)S(1)}, bf16[2,8,64,128]{3,2,1,0:T(8,128)(2,1)S(1)}, u32[]{:S(2)}, u32[]{:S(2)}) collective-permute-start(bf16[2,8,64,128]{3,2,1,0:T(8,128)(2,1)S(1)} %slice.12), channel_id=1, source_target_pairs={{0,4},{4,0},{8,12},{12,8},{1,5},{5,1},{9,13},{13,9},{2,6},{6,2},{1... | collective-permute-start | bytes 786440 | tf_op jit(solution)/shard_map/ppermute | solution.py:787
  50.1 1.9 %collective-permute-start.6 = (bf16[8,128,128]{2,1,0:T(8,128)(2,1)S(1)}, bf16[8,128,128]{2,1,0:T(8,128)(2,1)S(1)}, u32[]{:S(2)}, u32[]{:S(2)}) collective-permute-start(bf16[8,128,128]{2,1,0:T(8,128)(2,1)S(1)} %get-tuple-element.36), channel_id=1, source_target_pairs={{0,4},{4,8},{8,12},{1,5},{5,9},{9,13},{2,6},{6,10},{10,14},{3,7},{... | collective-permute-start | bytes 786440 | tf_op jit(solution)/shard_map/ppermute | solution.py:692
  52.1 4.7 %collective-permute-done.8.near_ref = bf16[2,8,64,128]{3,2,1,0:T(8,128)(2,1)S(1)} collective-permute-done((bf16[2,8,64,128]{3,2,1,0:T(8,128)(2,1)S(1)}, bf16[2,8,64,128]{3,2,1,0:T(8,128)(2,1)S(1)}, u32[]{:S(2)}, u32[]{:S(2)}) %collective-permute-start.8) | collective-permute-done | bytes 262176 | tf_op jit(solution)/shard_map/ppermute | solution.py:787
  56.8 2.6 %collective-permute-start.9 = (bf16[1,8,64,128]{3,2,1,0:T(8,128)(2,1)S(1)}, bf16[1,8,64,128]{3,2,1,0:T(8,128)(2,1)S(1)}, u32[]{:S(2)}, u32[]{:S(2)}) collective-permute-start(bf16[1,8,64,128]{3,2,1,0:T(8,128)(2,1)S(1)} %add_convert_fusion.1), channel_id=1, source_target_pairs={{0,8},{4,12},{8,0},{12,4},{1,9},{5,13},{9,1},{13,5},{2,10},{6,14},... | collective-permute-start | bytes 393224 | tf_op jit(solution)/shard_map/ppermute | solution.py:787
  60.1 0.7 %locals.1.local_ref = f32[4,16,8,128]{3,2,1,0:T(8,128)S(1)} custom-call(bf16[16,4,8,128]{3,2,1,0:T(8,128)(2,1)S(1)} %copy-done.3, bf16[16,4,8,128]{3,2,1,0:T(8,128)(2,1)S(1)} %copy-done.4, bf16[16,4,8,128]{3,2,1,0:T(8,128)(2,1)S(1)} %copy-done.7, bf16[4,8,16]{2,1,0:T(8,128)(2,1)S(1)} %bitcast.13, bf16[4,8,16]{2,1,0:T(8,128)(2,1)S(1)} %bitcast.15), custom_call_target="tpu_custom_call" | custom-call | tf_op jit(solution)/shard_map/locals/pallas_call | solution.py:472
  60.8 1.6 %collective-permute-done.6.entry_ref = bf16[8,128,128]{2,1,0:T(8,128)(2,1)S(1)} collective-permute-done((bf16[8,128,128]{2,1,0:T(8,128)(2,1)S(1)}, bf16[8,128,128]{2,1,0:T(8,128)(2,1)S(1)}, u32[]{:S(2)}, u32[]{:S(2)}) %collective-permute-start.6) | collective-permute-done | bytes 262176 | tf_op jit(solution)/shard_map/ppermute | solution.py:692
  62.4 2.6 %emit.1 = bf16[1024,8,128]{2,1,0:T(8,128)(2,1)} custom-call(f32[8,1024,128]{2,1,0:T(8,128)S(1)} %copy-done, bf16[8,1024,128]{2,1,0:T(8,128)(2,1)S(1)} %copy-done.1, bf16[8,128,128]{2,1,0:T(8,128)(2,1)S(1)} %collective-permute-done.6.entry_ref), custom_call_target="tpu_custom_call" | custom-call | flops 1000000000 | bytes 8388608 | tf_op jit(solution)/shard_map/emit/pallas_call | solution.py:643
  65.1 0.5 collective-permute-done.9.far_ref
  65.6 0.8 %finish.1 = bf16[16,4,8,128]{3,2,1,0:T(8,128)(2,1)} custom-call(s32[1]{0:T(128)S(6)} %copy.17.live, bf16[4,8,64,128]{3,2,1,0:T(8,128)(2,1)S(1)} %add_convert_fusion.mine_ref, bf16[2,8,64,128]{3,2,1,0:T(8,128)(2,1)S(1)} %collective-permute-done.8.near_ref, bf16[1,8,64,128]{3,2,1,0:T(8,128)(2,1)S(1)} %collective-permute-done.9.far_ref, ...), custom_call_target="tpu_custom_call" | custom-call | tf_op jit(solution)/shard_map/finish/pallas_call | solution.py:670
  (30 shorter events, 0.1 us)
Async XLA Ops:
  3.0 29.2 %collective-permute-start = (bf16[8,64,128]{2,1,0:T(8,128)(2,1)}, bf16[8,64,128]{2,1,0:T(8,128)(2,1)S(1)}, u32[]{:S(2)}, u32[]{:S(2)}) collective-permute-start(bf16[8,64,128]{2,1,0:T(8,128)(2,1)} %probes.1), channel_id=1, source_target_pairs={{0,8},{4,12},{8,0},{12,4},{1,9},{5,13},{9,1},{13,5},{2,10},{6,14},... | collective-permute-start | bytes 393224 | tf_op jit(solution)/shard_map/ppermute | solution.py:726
  7.0 25.1 %collective-permute-start.1 = (bf16[8,64,128]{2,1,0:T(8,128)(2,1)}, bf16[8,64,128]{2,1,0:T(8,128)(2,1)S(1)}, u32[]{:S(2)}, u32[]{:S(2)}) collective-permute-start(bf16[8,64,128]{2,1,0:T(8,128)(2,1)} %probes.1), channel_id=1, source_target_pairs={{0,4},{4,0},{8,12},{12,8},{1,5},{5,1},{9,13},{13,9},{2,6},{6,2},{1... | collective-permute-start | bytes 393224 | tf_op jit(solution)/shard_map/ppermute | solution.py:726
  8.6 23.6 %collective-permute-start.2 = (bf16[8,64,128]{2,1,0:T(8,128)(2,1)}, bf16[8,64,128]{2,1,0:T(8,128)(2,1)S(1)}, u32[]{:S(2)}, u32[]{:S(2)}) collective-permute-start(bf16[8,64,128]{2,1,0:T(8,128)(2,1)} %probes.1), channel_id=1, source_target_pairs={{0,12},{4,8},{8,4},{12,0},{1,13},{5,9},{9,5},{13,1},{2,14},{6,10},... | collective-permute-start | bytes 393224 | tf_op jit(solution)/shard_map/ppermute | solution.py:726
  8.6 23.6 %copy-start.12 = (bf16[8,64,128]{2,1,0:T(8,128)(2,1)S(1)}, bf16[8,64,128]{2,1,0:T(8,128)(2,1)}, u32[]{:S(2)}) copy-start(bf16[8,64,128]{2,1,0:T(8,128)(2,1)} %probes.1) | copy-start | bytes 393220
  8.6 26.3 %copy-start.13 = (s32[128]{0:T(128)S(1)}, s32[128]{0:T(128)}, u32[]{:S(2)}) copy-start(s32[128]{0:T(128)} %param.19) | copy-start | bytes 1540
  8.6 26.6 %copy-start.10 = (s32[1,4]{1,0:T(1,128)S(1)}, s32[1,4]{1,0:T(1,128)}, u32[]{:S(2)}) copy-start(s32[1,4]{1,0:T(1,128)} %lengths.5) | copy-start | bytes 52
  32.3 9.1 %copy-start.2 = (f32[8,128,128]{2,1,0:T(8,128)S(1)}, f32[8,128,128]{2,1,0:T(8,128)}, u32[]{:S(2)}) copy-start(f32[8,128,128]{2,1,0:T(8,128)} %get-tuple-element.24.state_ref) | copy-start | bytes 1572868
  32.3 9.1 %copy-start.5 = (bf16[8,128,128]{2,1,0:T(8,128)(2,1)S(1)}, bf16[8,128,128]{2,1,0:T(8,128)(2,1)}, u32[]{:S(2)}) copy-start(bf16[8,128,128]{2,1,0:T(8,128)(2,1)} %get-tuple-element.27.first_ref) | copy-start | bytes 786436
  32.3 9.0 %copy-start.6 = (bf16[8,128,128]{2,1,0:T(8,128)(2,1)S(1)}, bf16[8,128,128]{2,1,0:T(8,128)(2,1)}, u32[]{:S(2)}) copy-start(bf16[8,128,128]{2,1,0:T(8,128)(2,1)} %get-tuple-element.28.second_ref) | copy-start | bytes 786436
  32.3 2.9 %collective-permute-start.5 = (bf16[4,8,64,128]{3,2,1,0:T(8,128)(2,1)S(1)}, bf16[4,8,64,128]{3,2,1,0:T(8,128)(2,1)S(1)}, u32[]{:S(2)}, u32[]{:S(2)}) collective-permute-start(bf16[4,8,64,128]{3,2,1,0:T(8,128)(2,1)S(1)} %pad_maximum_fusion.own_ref), channel_id=1, source_target_pairs={{0,16},{16,0},{1,17},{17,1},{2,18},{18,2},{3,19},{19,3},{4,20},{20... | collective-permute-start | bytes 1572872 | tf_op jit(solution)/shard_map/ppermute | solution.py:760
  32.4 8.9 %collective-permute-start.3 = (bf16[8,128,128]{2,1,0:T(8,128)(2,1)}, bf16[8,128,128]{2,1,0:T(8,128)(2,1)S(1)}, u32[]{:S(2)}, u32[]{:S(2)}) collective-permute-start(bf16[8,128,128]{2,1,0:T(8,128)(2,1)} %get-tuple-element.27.first_ref), channel_id=1, source_target_pairs={{0,4},{4,0},{8,12},{12,8},{1,5},{5,1},{9,13},{13,9},{2,6},{6,2},{1... | collective-permute-start | bytes 786440 | tf_op jit(solution)/shard_map/ppermute | solution.py:740
  34.2 7.1 %collective-permute-start.4 = (bf16[8,128,128]{2,1,0:T(8,128)(2,1)}, bf16[8,128,128]{2,1,0:T(8,128)(2,1)S(1)}, u32[]{:S(2)}, u32[]{:S(2)}) collective-permute-start(bf16[8,128,128]{2,1,0:T(8,128)(2,1)} %get-tuple-element.28.second_ref), channel_id=1, source_target_pairs={{4,8},{8,4},{5,9},{9,5},{6,10},{10,6},{7,11},{11,7},{20,24},{24,20... | collective-permute-start | bytes 786440 | tf_op jit(solution)/shard_map/ppermute | solution.py:742
  35.2 1.2 %copy-start.11 = (bf16[4,8,128,128]{3,2,1,0:T(8,128)(2,1)S(1)}, bf16[4,8,128,128]{3,2,1,0:T(8,128)(2,1)}, u32[]{:S(2)}) copy-start(bf16[4,8,128,128]{3,2,1,0:T(8,128)(2,1)} %get-tuple-element.33.table_ref) | copy-start | bytes 3145732
  36.4 23.6 %copy-start.4 = (bf16[16,4,8,128]{3,2,1,0:T(8,128)(2,1)S(1)}, bf16[16,4,8,128]{3,2,1,0:T(8,128)(2,1)}, u32[]{:S(2)}) copy-start(bf16[16,4,8,128]{3,2,1,0:T(8,128)(2,1)} %k_ref.3) | copy-start | bytes 393220
  36.4 23.7 %copy-start.7 = (bf16[16,4,8,128]{3,2,1,0:T(8,128)(2,1)S(1)}, bf16[16,4,8,128]{3,2,1,0:T(8,128)(2,1)}, u32[]{:S(2)}) copy-start(bf16[16,4,8,128]{3,2,1,0:T(8,128)(2,1)} %v_ref) | copy-start | bytes 393220
  36.4 23.7 %copy-start.9 = (bf16[16,4,8]{0,2,1:T(8,128)(2,1)S(1)}, bf16[16,4,8]{0,2,1:T(8,128)(2,1)}, u32[]{:S(2)}) copy-start(bf16[16,4,8]{0,2,1:T(8,128)(2,1)} %param.25) | copy-start | bytes 3076
  41.4 21.1 %copy-start = (f32[8,1024,128]{2,1,0:T(8,128)S(1)}, f32[8,1024,128]{2,1,0:T(8,128)}, u32[]{:S(2)}) copy-start(f32[8,1024,128]{2,1,0:T(8,128)} %get-tuple-element.22.local_ref) | copy-start | bytes 12582916
  42.7 17.4 %copy-start.3 = (bf16[16,4,8,128]{3,2,1,0:T(8,128)(2,1)S(1)}, bf16[16,4,8,128]{3,2,1,0:T(8,128)(2,1)}, u32[]{:S(2)}) copy-start(bf16[16,4,8,128]{3,2,1,0:T(8,128)(2,1)} %q_ref.3) | copy-start | bytes 393220
  42.7 17.4 %copy-start.8 = (bf16[16,4,8]{0,2,1:T(8,128)(2,1)S(1)}, bf16[16,4,8]{0,2,1:T(8,128)(2,1)}, u32[]{:S(2)}) copy-start(bf16[16,4,8]{0,2,1:T(8,128)(2,1)} %param.24) | copy-start | bytes 3076
  42.7 19.7 %copy-start.1 = (bf16[8,1024,128]{2,1,0:T(8,128)(2,1)S(1)}, bf16[8,1024,128]{2,1,0:T(8,128)(2,1)}, u32[]{:S(2)}) copy-start(bf16[8,1024,128]{2,1,0:T(8,128)(2,1)} %get-tuple-element.23.probe_ref) | copy-start | bytes 6291460
  42.7 2.0 %collective-permute-start.7 = (bf16[4,8,64,128]{3,2,1,0:T(8,128)(2,1)S(1)}, bf16[4,8,64,128]{3,2,1,0:T(8,128)(2,1)S(1)}, u32[]{:S(2)}, u32[]{:S(2)}) collective-permute-start(bf16[4,8,64,128]{3,2,1,0:T(8,128)(2,1)S(1)} %get-tuple-element.38), channel_id=1, source_target_pairs={{0,16},{16,0},{1,17},{17,1},{2,18},{18,2},{3,19},{19,3},{4,20},{20... | collective-permute-start | bytes 1572872 | tf_op jit(solution)/shard_map/ppermute | solution.py:774
  44.9 11.9 %collective-permute-start.8 = (bf16[2,8,64,128]{3,2,1,0:T(8,128)(2,1)S(1)}, bf16[2,8,64,128]{3,2,1,0:T(8,128)(2,1)S(1)}, u32[]{:S(2)}, u32[]{:S(2)}) collective-permute-start(bf16[2,8,64,128]{3,2,1,0:T(8,128)(2,1)S(1)} %slice.12), channel_id=1, source_target_pairs={{0,4},{4,0},{8,12},{12,8},{1,5},{5,1},{9,13},{13,9},{2,6},{6,2},{1... | collective-permute-start | bytes 786440 | tf_op jit(solution)/shard_map/ppermute | solution.py:787
  50.1 12.3 %collective-permute-start.6 = (bf16[8,128,128]{2,1,0:T(8,128)(2,1)S(1)}, bf16[8,128,128]{2,1,0:T(8,128)(2,1)S(1)}, u32[]{:S(2)}, u32[]{:S(2)}) collective-permute-start(bf16[8,128,128]{2,1,0:T(8,128)(2,1)S(1)} %get-tuple-element.36), channel_id=1, source_target_pairs={{0,4},{4,8},{8,12},{1,5},{5,9},{9,13},{2,6},{6,10},{10,14},{3,7},{... | collective-permute-start | bytes 786440 | tf_op jit(solution)/shard_map/ppermute | solution.py:692
  56.8 8.7 %collective-permute-start.9 = (bf16[1,8,64,128]{3,2,1,0:T(8,128)(2,1)S(1)}, bf16[1,8,64,128]{3,2,1,0:T(8,128)(2,1)S(1)}, u32[]{:S(2)}, u32[]{:S(2)}) collective-permute-start(bf16[1,8,64,128]{3,2,1,0:T(8,128)(2,1)S(1)} %add_convert_fusion.1), channel_id=1, source_target_pairs={{0,8},{4,12},{8,0},{12,4},{1,9},{5,13},{9,1},{13,5},{2,10},{6,14},... | collective-permute-start | bytes 393224 | tf_op jit(solution)/shard_map/ppermute | solution.py:787

commit v4 on v2

--- a/solution.py
+++ b/solution.py
@@ -16,7 +16,7 @@
 SMALL_BYTES = 16 * MIB
 EMIT_BYTES = 20 * MIB
 CARRIED_MIB = 48
-EMIT_ROWS = 512
+EMIT_ROWS = 256
 BASE = 64
 SUBS = 2
 

time: 67.2 us -> 66.8 us (level)
  Pallas kernels: 33.7 us -> 37.1 us
  starting transfers between devices: 17.8 us -> 14.8 us
  waiting for transfers between devices: 12.1 us -> 11.4 us
    ppermute x2, starting transfers between devices: 8.56 us -> 6.2 us  [local(): before, theirs = (theirs, lax.ppermute(outgoing, 'dec', pairs))]
    pallas_call x1, Pallas kernels: 23.5 us -> 25.1 us  [prefill(): pl.pallas_call(functools.partial(chunk_kernel, tokens // SPAN), grid_spec...]
    pallas_call x1, Pallas kernels: 2.93 us -> 4.25 us  [stored_answers(): pl.pallas_call(functools.partial(stored_kernel, spans), grid_spec=pltpu.P...]
    ppermute x1, waiting for transfers between devices: 2.87 us -> 1.55 us  [local(): first_got = lax.ppermute(first, 'dec', pairs)]
    ppermute x1, starting transfers between devices: 0.91 us -> 0.07 us  [local(): first_got = lax.ppermute(first, 'dec', pairs)]
    ppermute x1, waiting for transfers between devices: 0.04 us -> 0.72 us  [local(): other_probes = lax.ppermute(own_probes, 'pre', [(0, 1), (1, 0)])]
  transfers between devices with their start and end apart: 10 -> 10, of which waited for: 5 -> 6; matrix products, arithmetic and copies ran while one was open for 0% -> 0% of each run, Pallas kernels for 44% -> 49%
where the time goes in v4:
time: 66.8 us; the launch traced here: 66.5 us
  Pallas kernels  37.1 us (56%)
  starting transfers between devices  14.8 us (22%)
  waiting for transfers between devices  11.4 us (17%)
  local copies, waits for them, and re-layouts  1.54 us (2%)
  between operations  1.49 us (2%)
    pallas_call x1, Pallas kernels, prefill(): pl.pallas_call(functools.partial(chunk_kernel, tokens // SPAN), grid_spec...  25.1 us
    ppermute x2, starting transfers between devices, local(): before, theirs = (theirs, lax.ppermute(outgoing, 'dec', pairs))  6.2 us
    ppermute x3, starting transfers between devices, local(): own_probes.append(lax.ppermute(probes, 'dec', pairs))  5.62 us
    ppermute x2, waiting for transfers between devices, local(): before, theirs = (theirs, lax.ppermute(outgoing, 'dec', pairs))  4.81 us
    pallas_call x1, Pallas kernels, stored_answers(): pl.pallas_call(functools.partial(stored_kernel, spans), grid_spec=pltpu.P...  4.25 us
    pallas_call x1, Pallas kernels, emit(): pl.pallas_call(emit_kernel, grid=(tokens // rows,), in_specs=[spec, spec,...  3.07 us
    pallas_call x1, Pallas kernels, requests(): pl.pallas_call(request_kernel, out_shape=[jax.ShapeDtypeStruct((heads, st...  2.56 us
    ppermute x1, waiting for transfers between devices, shifted(): lax.ppermute(array, 'dec', [(i, i + by) for i in range(peers) if 0 <= i +...  2.41 us
  transfers between devices with their start and end apart: 10, of which 6 were waited for; matrix products, arithmetic and copies ran while one was open for 0% of the time, Pallas kernels for 49%

profile of v4, /device:TPU:0, one launch (start us, length us, event | category | flops | bytes accessed | tf_op | source)
XLA Modules:
  0.0 66.5 jit_solution(3116993415509818177)
XLA Ops:
  0.6 2.6 %requests.1 = (bf16[8,64,128]{2,1,0:T(8,128)(2,1)}, f32[4,16,8,128]{3,2,1,0:T(8,128)}) custom-call(bf16[16,4,8,128]{3,2,1,0:T(8,128)(2,1)} %q_ref.1, bf16[16,4,8,128]{3,2,1,0:T(8,128)(2,1)} %k_ref.1, bf16[16,4,8,128]{3,2,1,0:T(8,128)(2,1)} %v_ref.1, bf16[4,8,16]{2,1,0:T(8,128)(2,1)} %bitcast.17, bf16[4,8,16]{2,1,0:T(8,128)(2,1)} %bitcast.18), custom_call_target="tpu_custom_call" | custom-call | tf_op jit(solution)/shard_map/requests/pallas_call | solution.py:463
  3.2 4.0 %collective-permute-start = (bf16[8,64,128]{2,1,0:T(8,128)(2,1)}, bf16[8,64,128]{2,1,0:T(8,128)(2,1)S(1)}, u32[]{:S(2)}, u32[]{:S(2)}) collective-permute-start(bf16[8,64,128]{2,1,0:T(8,128)(2,1)} %get-tuple-element.31), channel_id=1, source_target_pairs={{0,8},{4,12},{8,0},{12,4},{1,9},{5,13},{9,1},{13,5},{2,10},{6,14},... | collective-permute-start | bytes 393224 | tf_op jit(solution)/shard_map/ppermute | solution.py:719
  7.2 1.6 %collective-permute-start.1 = (bf16[8,64,128]{2,1,0:T(8,128)(2,1)}, bf16[8,64,128]{2,1,0:T(8,128)(2,1)S(1)}, u32[]{:S(2)}, u32[]{:S(2)}) collective-permute-start(bf16[8,64,128]{2,1,0:T(8,128)(2,1)} %get-tuple-element.31), channel_id=1, source_target_pairs={{0,4},{4,0},{8,12},{12,8},{1,5},{5,1},{9,13},{13,9},{2,6},{6,2},{1... | collective-permute-start | bytes 393224 | tf_op jit(solution)/shard_map/ppermute | solution.py:719
  8.8 0.0 collective-permute-start.2
  8.8 25.1 %chunks.1 = (f32[8,1024,128]{2,1,0:T(8,128)}, bf16[8,1024,128]{2,1,0:T(8,128)(2,1)}, f32[8,128,128]{2,1,0:T(8,128)}, bf16[8,128,128]{2,1,0:T(8,128)(2,1)}, bf16[...) custom-call(s32[1,4]{1,0:T(1,128)} %lengths.5, bf16[1024,8,128]{2,1,0:T(8,128)(2,1)} %bitcast.19, ...), custom_call_target="tpu_custom_call" | custom-call | flops 6000000000 | bytes 16777216 | tf_op jit(solution)/shard_map/chunks/pallas_call | solution.py:389
  33.9 0.0 collective-permute-done
  34.0 0.0 collective-permute-done.1
  34.0 0.0 collective-permute-done.2
  34.0 0.1 pad_maximum_fusion.own_ref
  34.1 0.1 collective-permute-start.5
  34.2 0.1 collective-permute-start.3
  34.2 0.8 %collective-permute-start.4 = (bf16[8,128,128]{2,1,0:T(8,128)(2,1)}, bf16[8,128,128]{2,1,0:T(8,128)(2,1)S(1)}, u32[]{:S(2)}, u32[]{:S(2)}) collective-permute-start(bf16[8,128,128]{2,1,0:T(8,128)(2,1)} %get-tuple-element.30.second_ref), channel_id=1, source_target_pairs={{4,8},{8,4},{5,9},{9,5},{6,10},{10,6},{7,11},{11,7},{20,24},{24,20... | collective-permute-start | bytes 786440 | tf_op jit(solution)/shard_map/ppermute | solution.py:732
  35.1 0.1 broadcast_in_dim.10
  35.2 0.2 reshape.10.source_ref
  35.3 0.7 %collective-permute-done.5.other_ref = bf16[4,8,64,128]{3,2,1,0:T(8,128)(2,1)S(1)} collective-permute-done((bf16[4,8,64,128]{3,2,1,0:T(8,128)(2,1)S(1)}, bf16[4,8,64,128]{3,2,1,0:T(8,128)(2,1)S(1)}, u32[]{:S(2)}, u32[]{:S(2)}) %collective-permute-start.5) | collective-permute-done | bytes 524320 | tf_op jit(solution)/shard_map/ppermute | solution.py:750
  36.1 1.2 %copy-done.7 = bf16[4,8,128,128]{3,2,1,0:T(8,128)(2,1)S(1)} copy-done((bf16[4,8,128,128]{3,2,1,0:T(8,128)(2,1)S(1)}, bf16[4,8,128,128]{3,2,1,0:T(8,128)(2,1)}, u32[]{:S(2)}) %copy-start.7) | copy-done | bytes 1048600
  37.3 4.3 %stored.1 = (bf16[4,8,64,128]{3,2,1,0:T(8,128)(2,1)S(1)}, bf16[4,8,64,128]{3,2,1,0:T(8,128)(2,1)S(1)}) custom-call(s32[1,4]{1,0:T(1,128)S(1)} %copy-done.6, bf16[4,8,128,128]{3,2,1,0:T(8,128)(2,1)S(1)} %copy-done.7, bf16[4,8,64,128]{3,2,1,0:T(8,128)(2,1)S(1)} %pad_maximum_fusion.own_ref, bf16[4,8,64,128]{3,2,1,0:T(8,128)(2,1)S(1)} %collective-permute-done.5.other_ref, ...), custom_call_target="tpu_custom_call" | custom-call | flops 1000000000 | bytes 16777216 | tf_op jit(solution)/shard_map/stored/pallas_call | solution.py:535
  41.6 1.5 %collective-permute-done.3.first_got_ref = bf16[8,128,128]{2,1,0:T(8,128)(2,1)S(1)} collective-permute-done((bf16[8,128,128]{2,1,0:T(8,128)(2,1)}, bf16[8,128,128]{2,1,0:T(8,128)(2,1)S(1)}, u32[]{:S(2)}, u32[]{:S(2)}) %collective-permute-start.3) | collective-permute-done | bytes 262176 | tf_op jit(solution)/shard_map/ppermute | solution.py:730
  43.1 0.0 collective-permute-done.4.second_got_ref
  43.1 1.3 %carried.1 = (bf16[8,128,128]{2,1,0:T(8,128)(2,1)S(1)}, bf16[4,8,64,128]{3,2,1,0:T(8,128)(2,1)S(1)}, bf16[4,8,64,128]{3,2,1,0:T(8,128)(2,1)S(1)}) custom-call(s32[1,4]{1,0:T(1,128)S(1)} %copy-done.6, f32[8,128,128]{2,1,0:T(8,128)S(1)} %copy-done.2, bf16[8,128,128]{2,1,0:T(8,128)(2,1)S(1)} %copy-done.4, bf16[8,128,128]{2,1,0:T(8,128)(2,1)S(1)} %copy-done.5, ...), custom_call_target="tpu_custom_call" | custom-call | tf_op jit(solution)/shard_map/carried/pallas_call | solution.py:612
  44.4 0.0 copy-start.1
  44.5 0.1 collective-permute-start.7
  44.5 1.9 %collective-permute-done.7 = bf16[4,8,64,128]{3,2,1,0:T(8,128)(2,1)S(1)} collective-permute-done((bf16[4,8,64,128]{3,2,1,0:T(8,128)(2,1)S(1)}, bf16[4,8,64,128]{3,2,1,0:T(8,128)(2,1)S(1)}, u32[]{:S(2)}, u32[]{:S(2)}) %collective-permute-start.7) | collective-permute-done | bytes 524320 | tf_op jit(solution)/shard_map/ppermute | solution.py:764
  46.4 0.2 add_convert_fusion.mine_ref
  46.6 3.7 %collective-permute-start.8 = (bf16[2,8,64,128]{3,2,1,0:T(8,128)(2,1)S(1)}, bf16[2,8,64,128]{3,2,1,0:T(8,128)(2,1)S(1)}, u32[]{:S(2)}, u32[]{:S(2)}) collective-permute-start(bf16[2,8,64,128]{3,2,1,0:T(8,128)(2,1)S(1)} %slice.12), channel_id=1, source_target_pairs={{0,4},{4,0},{8,12},{12,8},{1,5},{5,1},{9,13},{13,9},{2,6},{6,2},{1... | collective-permute-start | bytes 786440 | tf_op jit(solution)/shard_map/ppermute | solution.py:777
  50.3 1.9 %collective-permute-start.6 = (bf16[8,128,128]{2,1,0:T(8,128)(2,1)S(1)}, bf16[8,128,128]{2,1,0:T(8,128)(2,1)S(1)}, u32[]{:S(2)}, u32[]{:S(2)}) collective-permute-start(bf16[8,128,128]{2,1,0:T(8,128)(2,1)S(1)} %get-tuple-element.38), channel_id=1, source_target_pairs={{0,4},{4,8},{8,12},{1,5},{5,9},{9,13},{2,6},{6,10},{10,14},{3,7},{... | collective-permute-start | bytes 786440 | tf_op jit(solution)/shard_map/ppermute | solution.py:687
  52.3 4.7 %collective-permute-done.8.near_ref = bf16[2,8,64,128]{3,2,1,0:T(8,128)(2,1)S(1)} collective-permute-done((bf16[2,8,64,128]{3,2,1,0:T(8,128)(2,1)S(1)}, bf16[2,8,64,128]{3,2,1,0:T(8,128)(2,1)S(1)}, u32[]{:S(2)}, u32[]{:S(2)}) %collective-permute-start.8) | collective-permute-done | bytes 262176 | tf_op jit(solution)/shard_map/ppermute | solution.py:777
  57.0 2.5 %collective-permute-start.9 = (bf16[1,8,64,128]{3,2,1,0:T(8,128)(2,1)S(1)}, bf16[1,8,64,128]{3,2,1,0:T(8,128)(2,1)S(1)}, u32[]{:S(2)}, u32[]{:S(2)}) collective-permute-start(bf16[1,8,64,128]{3,2,1,0:T(8,128)(2,1)S(1)} %add_convert_fusion.1), channel_id=1, source_target_pairs={{0,8},{4,12},{8,0},{12,4},{1,9},{5,13},{9,1},{13,5},{2,10},{6,14},... | collective-permute-start | bytes 393224 | tf_op jit(solution)/shard_map/ppermute | solution.py:777
  60.2 2.4 %collective-permute-done.6.entry_ref = bf16[8,128,128]{2,1,0:T(8,128)(2,1)S(1)} collective-permute-done((bf16[8,128,128]{2,1,0:T(8,128)(2,1)S(1)}, bf16[8,128,128]{2,1,0:T(8,128)(2,1)S(1)}, u32[]{:S(2)}, u32[]{:S(2)}) %collective-permute-start.6) | collective-permute-done | bytes 262176 | tf_op jit(solution)/shard_map/ppermute | solution.py:687
  62.6 3.1 %emit.1 = bf16[1024,8,128]{2,1,0:T(8,128)(2,1)} custom-call(f32[8,1024,128]{2,1,0:T(8,128)S(1)} %copy-done, bf16[8,1024,128]{2,1,0:T(8,128)(2,1)S(1)} %copy-done.1, bf16[8,128,128]{2,1,0:T(8,128)(2,1)S(1)} %collective-permute-done.6.entry_ref), custom_call_target="tpu_custom_call" | custom-call | flops 1000000000 | bytes 8388608 | tf_op jit(solution)/shard_map/emit/pallas_call | solution.py:638
  65.7 0.1 collective-permute-done.9.far_ref
  65.8 0.8 %finish.1 = bf16[16,4,8,128]{3,2,1,0:T(8,128)(2,1)} custom-call(s32[1]{0:T(128)S(6)} %copy.17.live, bf16[4,8,64,128]{3,2,1,0:T(8,128)(2,1)S(1)} %add_convert_fusion.mine_ref, bf16[2,8,64,128]{3,2,1,0:T(8,128)(2,1)S(1)} %collective-permute-done.8.near_ref, bf16[1,8,64,128]{3,2,1,0:T(8,128)(2,1)S(1)} %collective-permute-done.9.far_ref, ...), custom_call_target="tpu_custom_call" | custom-call | tf_op jit(solution)/shard_map/finish/pallas_call | solution.py:665
  (21 shorter events, 0.1 us)
Async XLA Ops:
  3.2 30.8 %collective-permute-start = (bf16[8,64,128]{2,1,0:T(8,128)(2,1)}, bf16[8,64,128]{2,1,0:T(8,128)(2,1)S(1)}, u32[]{:S(2)}, u32[]{:S(2)}) collective-permute-start(bf16[8,64,128]{2,1,0:T(8,128)(2,1)} %get-tuple-element.31), channel_id=1, source_target_pairs={{0,8},{4,12},{8,0},{12,4},{1,9},{5,13},{9,1},{13,5},{2,10},{6,14},... | collective-permute-start | bytes 393224 | tf_op jit(solution)/shard_map/ppermute | solution.py:719
  7.2 26.7 %collective-permute-start.1 = (bf16[8,64,128]{2,1,0:T(8,128)(2,1)}, bf16[8,64,128]{2,1,0:T(8,128)(2,1)S(1)}, u32[]{:S(2)}, u32[]{:S(2)}) collective-permute-start(bf16[8,64,128]{2,1,0:T(8,128)(2,1)} %get-tuple-element.31), channel_id=1, source_target_pairs={{0,4},{4,0},{8,12},{12,8},{1,5},{5,1},{9,13},{13,9},{2,6},{6,2},{1... | collective-permute-start | bytes 393224 | tf_op jit(solution)/shard_map/ppermute | solution.py:719
  8.8 25.2 %collective-permute-start.2 = (bf16[8,64,128]{2,1,0:T(8,128)(2,1)}, bf16[8,64,128]{2,1,0:T(8,128)(2,1)S(1)}, u32[]{:S(2)}, u32[]{:S(2)}) collective-permute-start(bf16[8,64,128]{2,1,0:T(8,128)(2,1)} %get-tuple-element.31), channel_id=1, source_target_pairs={{0,12},{4,8},{8,4},{12,0},{1,13},{5,9},{9,5},{13,1},{2,14},{6,10},... | collective-permute-start | bytes 393224 | tf_op jit(solution)/shard_map/ppermute | solution.py:719
  8.8 25.2 %copy-start.8 = (bf16[8,64,128]{2,1,0:T(8,128)(2,1)S(1)}, bf16[8,64,128]{2,1,0:T(8,128)(2,1)}, u32[]{:S(2)}) copy-start(bf16[8,64,128]{2,1,0:T(8,128)(2,1)} %get-tuple-element.31) | copy-start | bytes 393220
  8.8 26.3 %copy-start.9 = (s32[128]{0:T(128)S(1)}, s32[128]{0:T(128)}, u32[]{:S(2)}) copy-start(s32[128]{0:T(128)} %param.19) | copy-start | bytes 1540
  8.8 27.3 %copy-start.6 = (s32[1,4]{1,0:T(1,128)S(1)}, s32[1,4]{1,0:T(1,128)}, u32[]{:S(2)}) copy-start(s32[1,4]{1,0:T(1,128)} %lengths.5) | copy-start | bytes 52
  34.1 9.0 %copy-start.2 = (f32[8,128,128]{2,1,0:T(8,128)S(1)}, f32[8,128,128]{2,1,0:T(8,128)}, u32[]{:S(2)}) copy-start(f32[8,128,128]{2,1,0:T(8,128)} %get-tuple-element.26.state_ref) | copy-start | bytes 1572868
  34.1 9.0 %copy-start.4 = (bf16[8,128,128]{2,1,0:T(8,128)(2,1)S(1)}, bf16[8,128,128]{2,1,0:T(8,128)(2,1)}, u32[]{:S(2)}) copy-start(bf16[8,128,128]{2,1,0:T(8,128)(2,1)} %get-tuple-element.29.first_ref) | copy-start | bytes 786436
  34.1 9.0 %copy-start.5 = (bf16[8,128,128]{2,1,0:T(8,128)(2,1)S(1)}, bf16[8,128,128]{2,1,0:T(8,128)(2,1)}, u32[]{:S(2)}) copy-start(bf16[8,128,128]{2,1,0:T(8,128)(2,1)} %get-tuple-element.30.second_ref) | copy-start | bytes 786436
  34.1 2.0 %collective-permute-start.5 = (bf16[4,8,64,128]{3,2,1,0:T(8,128)(2,1)S(1)}, bf16[4,8,64,128]{3,2,1,0:T(8,128)(2,1)S(1)}, u32[]{:S(2)}, u32[]{:S(2)}) collective-permute-start(bf16[4,8,64,128]{3,2,1,0:T(8,128)(2,1)S(1)} %pad_maximum_fusion.own_ref), channel_id=1, source_target_pairs={{0,16},{16,0},{1,17},{17,1},{2,18},{18,2},{3,19},{19,3},{4,20},{20... | collective-permute-start | bytes 1572872 | tf_op jit(solution)/shard_map/ppermute | solution.py:750
  34.2 8.9 %collective-permute-start.3 = (bf16[8,128,128]{2,1,0:T(8,128)(2,1)}, bf16[8,128,128]{2,1,0:T(8,128)(2,1)S(1)}, u32[]{:S(2)}, u32[]{:S(2)}) collective-permute-start(bf16[8,128,128]{2,1,0:T(8,128)(2,1)} %get-tuple-element.29.first_ref), channel_id=1, source_target_pairs={{0,4},{4,0},{8,12},{12,8},{1,5},{5,1},{9,13},{13,9},{2,6},{6,2},{1... | collective-permute-start | bytes 786440 | tf_op jit(solution)/shard_map/ppermute | solution.py:730
  34.2 8.9 %collective-permute-start.4 = (bf16[8,128,128]{2,1,0:T(8,128)(2,1)}, bf16[8,128,128]{2,1,0:T(8,128)(2,1)S(1)}, u32[]{:S(2)}, u32[]{:S(2)}) collective-permute-start(bf16[8,128,128]{2,1,0:T(8,128)(2,1)} %get-tuple-element.30.second_ref), channel_id=1, source_target_pairs={{4,8},{8,4},{5,9},{9,5},{6,10},{10,6},{7,11},{11,7},{20,24},{24,20... | collective-permute-start | bytes 786440 | tf_op jit(solution)/shard_map/ppermute | solution.py:732
  36.1 1.2 %copy-start.7 = (bf16[4,8,128,128]{3,2,1,0:T(8,128)(2,1)S(1)}, bf16[4,8,128,128]{3,2,1,0:T(8,128)(2,1)}, u32[]{:S(2)}) copy-start(bf16[4,8,128,128]{3,2,1,0:T(8,128)(2,1)} %get-tuple-element.35.table_ref) | copy-start | bytes 3145732
  43.1 19.5 %copy-start = (f32[8,1024,128]{2,1,0:T(8,128)S(1)}, f32[8,1024,128]{2,1,0:T(8,128)}, u32[]{:S(2)}) copy-start(f32[8,1024,128]{2,1,0:T(8,128)} %get-tuple-element.24.local_ref) | copy-start | bytes 12582916
  44.4 18.2 %copy-start.1 = (bf16[8,1024,128]{2,1,0:T(8,128)(2,1)S(1)}, bf16[8,1024,128]{2,1,0:T(8,128)(2,1)}, u32[]{:S(2)}) copy-start(bf16[8,1024,128]{2,1,0:T(8,128)(2,1)} %get-tuple-element.25.probe_ref) | copy-start | bytes 6291460
  44.5 2.0 %collective-permute-start.7 = (bf16[4,8,64,128]{3,2,1,0:T(8,128)(2,1)S(1)}, bf16[4,8,64,128]{3,2,1,0:T(8,128)(2,1)S(1)}, u32[]{:S(2)}, u32[]{:S(2)}) collective-permute-start(bf16[4,8,64,128]{3,2,1,0:T(8,128)(2,1)S(1)} %get-tuple-element.40), channel_id=1, source_target_pairs={{0,16},{16,0},{1,17},{17,1},{2,18},{18,2},{3,19},{19,3},{4,20},{20... | collective-permute-start | bytes 1572872 | tf_op jit(solution)/shard_map/ppermute | solution.py:764
  46.6 10.3 %collective-permute-start.8 = (bf16[2,8,64,128]{3,2,1,0:T(8,128)(2,1)S(1)}, bf16[2,8,64,128]{3,2,1,0:T(8,128)(2,1)S(1)}, u32[]{:S(2)}, u32[]{:S(2)}) collective-permute-start(bf16[2,8,64,128]{3,2,1,0:T(8,128)(2,1)S(1)} %slice.12), channel_id=1, source_target_pairs={{0,4},{4,0},{8,12},{12,8},{1,5},{5,1},{9,13},{13,9},{2,6},{6,2},{1... | collective-permute-start | bytes 786440 | tf_op jit(solution)/shard_map/ppermute | solution.py:777
  50.3 12.3 %collective-permute-start.6 = (bf16[8,128,128]{2,1,0:T(8,128)(2,1)S(1)}, bf16[8,128,128]{2,1,0:T(8,128)(2,1)S(1)}, u32[]{:S(2)}, u32[]{:S(2)}) collective-permute-start(bf16[8,128,128]{2,1,0:T(8,128)(2,1)S(1)} %get-tuple-element.38), channel_id=1, source_target_pairs={{0,4},{4,8},{8,12},{1,5},{5,9},{9,13},{2,6},{6,10},{10,14},{3,7},{... | collective-permute-start | bytes 786440 | tf_op jit(solution)/shard_map/ppermute | solution.py:687
  57.0 8.7 %collective-permute-start.9 = (bf16[1,8,64,128]{3,2,1,0:T(8,128)(2,1)S(1)}, bf16[1,8,64,128]{3,2,1,0:T(8,128)(2,1)S(1)}, u32[]{:S(2)}, u32[]{:S(2)}) collective-permute-start(bf16[1,8,64,128]{3,2,1,0:T(8,128)(2,1)S(1)} %add_convert_fusion.1), channel_id=1, source_target_pairs={{0,8},{4,12},{8,0},{12,4},{1,9},{5,13},{9,1},{13,5},{2,10},{6,14},... | collective-permute-start | bytes 393224 | tf_op jit(solution)/shard_map/ppermute | solution.py:777
  62.6 3.2 %copy-start.3 = (f32[4,16,8,128]{3,2,1,0:T(8,128)S(1)}, f32[4,16,8,128]{3,2,1,0:T(8,128)}, u32[]{:S(2)}) copy-start(f32[4,16,8,128]{3,2,1,0:T(8,128)} %get-tuple-element.41.local_ref) | copy-start | bytes 786436
